TPU v7x, 32 devices: a whole 2x2x4 slice. The times are simulated.
32 devices in a mesh: dp: 8 (over z, x), ctx: 4 (over y, core).
Axes of the slice: x: 2, y: 2, z: 4, core: 2. Of those that a mesh axis runs over, the one named last changes fastest.
Arguments:
- tokens: bfloat16 [8, 512, 640], P('dp', 'ctx'), may hold values from -6 to 6
- cotangent: bfloat16 [8, 512, 640], P('dp', 'ctx'), may hold values from -6 to 6
- segments: int32 [8, 512], P('dp', 'ctx'), may hold values from 0 to 3, never falling along the last dimension, each value on 1 to 384 neighbouring positions
- gains: bfloat16 [3072], P(('dp', 'ctx')), may hold values from 0.5 to 1.5
- w_query: bfloat16 [640, 1024], P(None, ('dp', 'ctx')), may hold values from -0.25 to 0.25
- w_key: bfloat16 [640, 256], P(None, ('dp', 'ctx')), may hold values from -0.25 to 0.25
- w_value: bfloat16 [640, 256], P(None, ('dp', 'ctx')), may hold values from -0.25 to 0.25
- w_out: bfloat16 [1024, 640], P(('dp', 'ctx')), may hold values from -0.1875 to 0.1875
- w_gate: bfloat16 [640, 2048], P(None, ('dp', 'ctx')), may hold values from -0.25 to 0.25
- w_up: bfloat16 [640, 2048], P(None, ('dp', 'ctx')), may hold values from -0.25 to 0.25
- w_down: bfloat16 [2048, 640], P(('dp', 'ctx')), may hold values from -0.125 to 0.125
Outputs:
- mixed: bfloat16 [8, 512, 640], P('dp', 'ctx')
- tokens_grad: bfloat16 [8, 512, 640], P('dp', 'ctx')
- gains_grad: float32 [3072], P(('dp', 'ctx'))
- w_query_grad: float32 [640, 1024], P(None, ('dp', 'ctx'))
- w_key_grad: float32 [640, 256], P(None, ('dp', 'ctx'))
- w_value_grad: float32 [640, 256], P(None, ('dp', 'ctx'))
- w_out_grad: float32 [1024, 640], P(('dp', 'ctx'))
- w_gate_grad: float32 [640, 2048], P(None, ('dp', 'ctx'))
- w_up_grad: float32 [640, 2048], P(None, ('dp', 'ctx'))
- w_down_grad: float32 [2048, 640], P(('dp', 'ctx'))
Inputs may be any that keep to these rules, and one draw needn't show every extreme that they name: `segments`: each sequence holds 4 documents numbered in order, each of 1 to 384 tokens, one of exactly 384.
All inputs are finite; a program needn't handle non-finite values.
Results may differ from a plain program's by a relative error of at most 0.015.
Values may be sent and summed in bfloat16 or wider, within the bound.
A program may use at most 128 MiB of HBM per device.

v0:
```python
import jax
import jax.numpy as jnp
from jax import lax
from jax.sharding import PartitionSpec as P

D = 640
H = 4
HD = 256


EPS = 1e-06
ROPE_BASE = 1000000.0
NEGATIVE = -1e30


def norm_forward(value, gain):
    factor = lax.rsqrt(jnp.mean(value * value, axis=-1, keepdims=True) + EPS)
    return (value * factor * gain, factor)


def norm_backward(value, factor, gain, grad_out):
    scaled = grad_out * gain
    grad_in = factor * scaled - value * (factor * factor * factor) * jnp.mean(
        scaled * value, axis=-1, keepdims=True
    )
    grad_gain = jnp.sum((grad_out * value * factor).reshape(-1, value.shape[-1]), axis=0)
    return (grad_in, grad_gain)


def rotary_tables(positions, width):
    exponent = jnp.arange(0, width, 2, dtype=jnp.int32).astype(jnp.float32) / width
    freqs = jnp.power(jnp.float32(ROPE_BASE), -exponent)
    theta = positions.astype(jnp.float32)[:, None] * freqs[None, :]
    return (jnp.cos(theta), jnp.sin(theta))


def rotate(value, cosine, sine):
    half = value.shape[-1] // 2
    first = value[..., :half]
    second = value[..., half:]
    return jnp.concatenate(
        [first * cosine - second * sine, second * cosine + first * sine], axis=-1
    )


def product(left, right):
    return jnp.dot(left, right, preferred_element_type=jnp.float32)


def inner_rows(left, right):
    return lax.dot_general(
        left, right, (((0,), (0,)), ((), ())), preferred_element_type=jnp.float32
    )


def against(left, right):
    return lax.dot_general(
        left, right, (((1,), (1,)), ((), ())), preferred_element_type=jnp.float32
    )


def gelu_mix(gate_in, up_in):
    return jax.nn.gelu(gate_in, approximate=True) * up_in


def owner_blocks(term, layout, groups, cycle):
    if layout == "col":
        return term.reshape(term.shape[0], groups, cycle, term.shape[1] // (groups * cycle))
    if layout == "row":
        return term.reshape(1, groups, cycle, term.shape[0] // (groups * cycle) * term.shape[1])
    return term.reshape(1, groups, cycle, term.shape[0] // (groups * cycle))


def shard_back(block, layout, whole):
    if layout == "col":
        return block.reshape(whole[0], -1)
    if layout == "row":
        return block.reshape(-1, whole[1])
    return block.reshape(-1)


def body(tokens, cotangent, segments, gains, w_query, w_key, w_value, w_out, w_gate, w_up, w_down):
    resid = tokens[0].astype(jnp.float32)
    rows = resid.shape[0]
    cycle = lax.axis_size("ctx")
    groups = lax.axis_size("dp")
    place = lax.axis_index("ctx")
    scale = HD ** (-0.5)
    doc_local = segments[0]
    doc_all = lax.all_gather(doc_local, "ctx", axis=0, tiled=True)
    shards = (w_query, w_key, w_value, w_out, w_gate, w_up, w_down, gains)
    gathered = (
        lax.all_gather(shards[0], ("dp", "ctx"), axis=1, tiled=True),
        lax.all_gather(shards[1], ("dp", "ctx"), axis=1, tiled=True),
        lax.all_gather(shards[2], ("dp", "ctx"), axis=1, tiled=True),
        lax.all_gather(shards[3], ("dp", "ctx"), axis=0, tiled=True),
        lax.all_gather(shards[4], ("dp", "ctx"), axis=1, tiled=True),
        lax.all_gather(shards[5], ("dp", "ctx"), axis=1, tiled=True),
        lax.all_gather(shards[6], ("dp", "ctx"), axis=0, tiled=True),
        lax.all_gather(shards[7], ("dp", "ctx"), axis=0, tiled=True),
    )
    full_query, full_key, full_value, full_out, full_gate, full_up, full_down, full_gains = gathered
    gain_all = full_gains.astype(jnp.float32)
    g_in = gain_all[0:D]
    g_post_attn = gain_all[D : 2 * D]
    g_pre_ff = gain_all[2 * D : 3 * D]
    g_post_ff = gain_all[3 * D : 4 * D]
    g_query = gain_all[4 * D : 4 * D + HD]
    g_key = gain_all[4 * D + HD : 4 * D + 2 * HD]
    normed_f, in_factor = norm_forward(resid, g_in)
    normed = normed_f.astype(jnp.bfloat16)
    queries = product(normed, full_query).reshape(rows, H, HD)
    keys = product(normed, full_key)
    values = product(normed, full_value).astype(jnp.bfloat16)
    positions = place * rows + jnp.arange(rows, dtype=jnp.int32)
    cosine, sine = rotary_tables(positions, HD)
    query_normed, query_factor = norm_forward(queries, g_query)
    key_normed, key_factor = norm_forward(keys, g_key)
    query_rot = (rotate(query_normed, cosine[:, None, :], sine[:, None, :]) * scale).astype(
        jnp.bfloat16
    )
    key_rot = rotate(key_normed, cosine, sine).astype(jnp.bfloat16)
    query_rows = jnp.transpose(query_rot, (1, 0, 2)).reshape(H * rows, HD)
    query_pos = jnp.tile(positions, H)
    query_doc = jnp.tile(doc_local, H)

    def scores_for(piece_keys):
        count = piece_keys.shape[0]
        logits = against(query_rows, piece_keys)
        key_pos = jnp.arange(count, dtype=jnp.int32)
        allowed = (key_pos[None, :] <= query_pos[:, None]) & (
            doc_all[None, :] == query_doc[:, None]
        )
        return (logits, allowed)

    piece = (
        lax.all_gather(key_rot, "ctx", axis=0, tiled=True),
        lax.all_gather(values, "ctx", axis=0, tiled=True),
    )
    top = jnp.full((H * rows,), NEGATIVE, jnp.float32)
    logits, allowed = scores_for(piece[0])
    masked = jnp.where(allowed, logits, NEGATIVE)
    new_top = jnp.maximum(top, jnp.max(masked, axis=1))
    weights = jnp.where(allowed, jnp.exp(masked - new_top[:, None]), 0.0)
    total = jnp.sum(weights, axis=1)
    accum = jnp.dot(weights, piece[1].astype(jnp.float32), precision=lax.Precision.HIGHEST)
    top, total, accum = (new_top, total, accum)
    log_total = top + jnp.log(total)
    attended_rows = accum / total[:, None]
    attended = jnp.transpose(attended_rows.reshape(H, rows, HD), (1, 0, 2))
    heads = attended.reshape(rows, H * HD).astype(jnp.bfloat16)
    branch = product(heads, full_out)
    attn_normed, branch_factor = norm_forward(branch, g_post_attn)
    hidden = resid + attn_normed
    ff_f, ff_factor = norm_forward(hidden, g_pre_ff)
    ff_in = ff_f.astype(jnp.bfloat16)
    gate = product(ff_in, full_gate)
    up_proj = product(ff_in, full_up)
    mid = gelu_mix(gate, up_proj).astype(jnp.bfloat16)
    down = product(mid, full_down)
    down_normed, down_factor = norm_forward(down, g_post_ff)
    mixed = (hidden + down_normed).astype(jnp.bfloat16)
    back = (
        lax.all_gather(shards[0], ("dp", "ctx"), axis=1, tiled=True),
        lax.all_gather(shards[1], ("dp", "ctx"), axis=1, tiled=True),
        lax.all_gather(shards[2], ("dp", "ctx"), axis=1, tiled=True),
        lax.all_gather(shards[3], ("dp", "ctx"), axis=0, tiled=True),
        lax.all_gather(shards[4], ("dp", "ctx"), axis=1, tiled=True),
        lax.all_gather(shards[5], ("dp", "ctx"), axis=1, tiled=True),
        lax.all_gather(shards[6], ("dp", "ctx"), axis=0, tiled=True),
        lax.all_gather(shards[7], ("dp", "ctx"), axis=0, tiled=True),
    )
    back_query, back_key, back_value, back_out, back_gate, back_up, back_down, back_gains = back
    grad_out = cotangent[0].astype(jnp.float32)
    grad_down_f, grad_g_post_ff = norm_backward(down, down_factor, g_post_ff, grad_out)
    grad_down = grad_down_f.astype(jnp.bfloat16)
    w_down_part = inner_rows(mid, grad_down)
    grad_mid = against(grad_down, back_down)
    _, gelu_back = jax.vjp(gelu_mix, gate, up_proj)
    grad_gate_f, grad_up_f = gelu_back(grad_mid)
    grad_gate = grad_gate_f.astype(jnp.bfloat16)
    grad_up = grad_up_f.astype(jnp.bfloat16)
    w_gate_part = inner_rows(ff_in, grad_gate)
    w_up_part = inner_rows(ff_in, grad_up)
    grad_ff = against(grad_gate, back_gate) + against(grad_up, back_up)
    hidden_part, grad_g_pre_ff = norm_backward(hidden, ff_factor, g_pre_ff, grad_ff)
    grad_hidden = grad_out + hidden_part
    grad_branch_f, grad_g_post_attn = norm_backward(branch, branch_factor, g_post_attn, grad_hidden)
    grad_branch = grad_branch_f.astype(jnp.bfloat16)
    w_out_part = inner_rows(heads, grad_branch)
    feed_layouts = ("row", "col", "col", "row")
    feed_terms = (w_out_part, w_gate_part, w_up_part, w_down_part)
    grad_att = against(grad_branch, back_out).reshape(rows, H, HD).astype(jnp.bfloat16)
    grad_rows = jnp.transpose(grad_att, (1, 0, 2)).reshape(H * rows, HD)
    delta = jnp.sum(grad_rows.astype(jnp.float32) * attended_rows, axis=1)
    piece = (
        lax.all_gather(key_rot, "ctx", axis=0, tiled=True),
        lax.all_gather(values, "ctx", axis=0, tiled=True),
    )
    logits, allowed = scores_for(piece[0])
    probs = jnp.where(
        allowed, jnp.exp(jnp.where(allowed, logits, NEGATIVE) - log_total[:, None]), 0.0
    )
    probs_low = probs.astype(jnp.bfloat16)
    grad_probs = against(grad_rows, piece[1])
    grad_logits = (probs * (grad_probs - delta[:, None])).astype(jnp.bfloat16)
    grad_query = product(grad_logits, piece[0])
    grad_key_part = inner_rows(grad_logits, query_rows)
    grad_value_part = inner_rows(probs_low, grad_rows)
    count = piece[0].shape[0]
    updated = jnp.concatenate([grad_key_part, grad_value_part], axis=1)
    grad_kv = updated
    grad_qrows, grad_kv = (grad_query, grad_kv)
    key_grad = lax.psum_scatter(grad_kv, "ctx", scatter_dimension=0, tiled=True)
    grad_krot = key_grad[:, :HD]
    grad_values = key_grad[:, HD:].astype(jnp.bfloat16)
    grad_qrot = jnp.transpose(grad_qrows.reshape(H, rows, HD), (1, 0, 2))
    grad_qn = rotate(grad_qrot * scale, cosine[:, None, :], -sine[:, None, :])
    grad_queries_f, grad_g_query = norm_backward(queries, query_factor, g_query, grad_qn)
    grad_queries = grad_queries_f.reshape(rows, H * HD).astype(jnp.bfloat16)
    grad_kn = rotate(grad_krot, cosine, -sine)
    grad_keys_f, grad_g_key = norm_backward(keys, key_factor, g_key, grad_kn)
    grad_keys = grad_keys_f.astype(jnp.bfloat16)
    w_query_part = inner_rows(normed, grad_queries)
    w_key_part = inner_rows(normed, grad_keys)
    w_value_part = inner_rows(normed, grad_values)
    grad_normed = (
        against(grad_queries, back_query)
        + against(grad_keys, back_key)
        + against(grad_values, back_value)
    )
    input_part, grad_g_in = norm_backward(resid, in_factor, g_in, grad_normed)
    tokens_grad = (grad_hidden + input_part).astype(jnp.bfloat16)
    gains_part = jnp.concatenate(
        [grad_g_in, grad_g_post_attn, grad_g_pre_ff, grad_g_post_ff, grad_g_query, grad_g_key]
    )
    attn_layouts = ("col", "col", "col", "vec")
    attn_terms = (w_query_part, w_key_part, w_value_part, gains_part)
    every_terms = attn_terms + feed_terms
    every_layouts = attn_layouts + feed_layouts
    blocks = [
        owner_blocks(term, layout, groups, cycle)
        for term, layout in zip(every_terms, every_layouts)
    ]
    moved = (
        lax.all_to_all(blocks[0], "ctx", split_axis=2, concat_axis=2, tiled=True),
        lax.all_to_all(blocks[1], "ctx", split_axis=2, concat_axis=2, tiled=True),
        lax.all_to_all(blocks[2], "ctx", split_axis=2, concat_axis=2, tiled=True),
        lax.all_to_all(blocks[3], "ctx", split_axis=2, concat_axis=2, tiled=True),
        lax.all_to_all(blocks[4], "ctx", split_axis=2, concat_axis=2, tiled=True),
        lax.all_to_all(blocks[5], "ctx", split_axis=2, concat_axis=2, tiled=True),
        lax.all_to_all(blocks[6], "ctx", split_axis=2, concat_axis=2, tiled=True),
        lax.all_to_all(blocks[7], "ctx", split_axis=2, concat_axis=2, tiled=True),
    )
    local = [jnp.sum(block, axis=2) for block in moved]
    reduced = (
        lax.psum_scatter(local[0], "dp", scatter_dimension=1, tiled=True),
        lax.psum_scatter(local[1], "dp", scatter_dimension=1, tiled=True),
        lax.psum_scatter(local[2], "dp", scatter_dimension=1, tiled=True),
        lax.psum_scatter(local[3], "dp", scatter_dimension=1, tiled=True),
        lax.psum_scatter(local[4], "dp", scatter_dimension=1, tiled=True),
        lax.psum_scatter(local[5], "dp", scatter_dimension=1, tiled=True),
        lax.psum_scatter(local[6], "dp", scatter_dimension=1, tiled=True),
        lax.psum_scatter(local[7], "dp", scatter_dimension=1, tiled=True),
    )
    every_terms = attn_terms + feed_terms
    every_layouts = attn_layouts + feed_layouts
    owned = [
        shard_back(block, layout, term.shape)
        for block, layout, term in zip(reduced, every_layouts, every_terms)
    ]
    return (
        mixed[None],
        tokens_grad[None],
        owned[3],
        owned[0],
        owned[1],
        owned[2],
        owned[4],
        owned[5],
        owned[6],
        owned[7],
    )


def solution(mesh):
    return jax.shard_map(
        body,
        mesh=mesh,
        in_specs=(
            P("dp", "ctx", None),
            P("dp", "ctx", None),
            P("dp", "ctx"),
            P(("dp", "ctx")),
            P(None, ("dp", "ctx")),
            P(None, ("dp", "ctx")),
            P(None, ("dp", "ctx")),
            P(("dp", "ctx"), None),
            P(None, ("dp", "ctx")),
            P(None, ("dp", "ctx")),
            P(("dp", "ctx"), None),
        ),
        out_specs=(
            P("dp", "ctx", None),
            P("dp", "ctx", None),
            P(("dp", "ctx")),
            P(None, ("dp", "ctx")),
            P(None, ("dp", "ctx")),
            P(None, ("dp", "ctx")),
            P(("dp", "ctx"), None),
            P(None, ("dp", "ctx")),
            P(None, ("dp", "ctx")),
            P(("dp", "ctx"), None),
        ),
        check_vma=False,
    )
```

profile of v0, /device:TPU:0, one launch (start us, length us, event | category | flops | bytes accessed | tf_op | source)
XLA Modules:
  0.0 903.0 jit_solution(2644064846549777144)
XLA Ops:
  11.5 42.1 %all-reduce = bf16[3072]{0:T(1024)(128)(2,1)S(1)} all-reduce(bf16[3072]{0:T(1024)(128)(2,1)S(1)} %dynamic-update-slice), channel_id=1, replica_groups=mesh['dp'=8,'ctx'=4] {'dp','ctx'}, use_global_device_ids=true, to_apply=%add | all-reduce | flops 3072 | bytes 12288
  55.3 41.4 %all_gather.45 = bf16[640,256]{0,1:T(8,128)(2,1)S(1)} all-gather(bf16[640,8]{0,1:T(8,128)(2,1)} %param.16), channel_id=1, replica_groups=mesh['dp'=8,'ctx'=4] {'dp','ctx'}, dimensions={1}, use_global_device_ids=true | all-gather | bytes 337920 | tf_op jit(solution)/shard_map/all_gather | solution.py:94
  99.3 5.2 all-gather
  104.9 5.8 all_gather.46
  110.7 38.1 %all_gather.47 = bf16[640,256]{0,1:T(8,128)(2,1)S(1)} all-gather(bf16[640,8]{0,1:T(8,128)(2,1)} %param.17), channel_id=1, replica_groups=mesh['dp'=8,'ctx'=4] {'dp','ctx'}, dimensions={1}, use_global_device_ids=true | all-gather | bytes 337920 | tf_op jit(solution)/shard_map/all_gather | solution.py:95
  149.7 7.2 all_gather.48
  157.0 2.0 multiply_reduce_fusion.3
  161.3 2.0 fusion.88
  163.5 1.9 multiply_reduce_fusion.10
  165.8 18.6 %all-gather.11.cloned.1.call-done = bf16[640,2048]{0,1:T(8,128)(2,1)} async-done(((bf16[640,64]{0,1:T(8,128)(2,1)}), bf16[640,2048]{0,1:T(8,128)(2,1)}) %all-gather.11.cloned.1.call-update) | async-done | bytes 2621456 | tf_op jit(solution)/shard_map/all_gather | solution.py:97
  184.4 3.7 fusion.89
  188.1 56.0 %all-gather.13.cloned.1.call-done = bf16[640,2048]{0,1:T(8,128)(2,1)} async-done(((bf16[640,64]{0,1:T(8,128)(2,1)}), bf16[640,2048]{0,1:T(8,128)(2,1)}) %all-gather.13.cloned.1.call-update) | async-done | bytes 2621456 | tf_op jit(solution)/shard_map/all_gather | solution.py:98
  244.1 4.0 multiply_convert_fusion.1
  248.0 55.7 %all-gather.15.cloned.1.call-done = bf16[2048,640]{1,0:T(8,128)(2,1)} async-done(((bf16[64,640]{1,0:T(8,128)(2,1)}), bf16[2048,640]{1,0:T(8,128)(2,1)}) %all-gather.15.cloned.1.call-update) | async-done | bytes 2621456 | tf_op jit(solution)/shard_map/all_gather | solution.py:99
  303.7 2.6 multiply_reduce_fusion.8
  307.3 1.4 multiply_convert_fusion
  317.3 1.5 fusion.93
  318.8 2.4 reshape.368
  321.2 4.8 copy.66
  326.0 3.7 all-to-all-start.4
  329.7 17.2 %reduce-scatter.14.cloned.1.call-done = f32[128,512]{1,0:T(8,128)} async-done(((f32[512,512]{1,0:T(8,128)}), f32[128,512]{1,0:T(8,128)}) %reduce-scatter.14.cloned.1.call-update) | async-done | bytes 262160 | tf_op jit(solution)/shard_map/reduce_scatter | solution.py:214
  346.9 1.8 fusion.66
  348.7 1.6 multiply_reduce_fusion.11
  350.3 1.7 subtract_convert_fusion.2
  352.0 1.6 copy.62
  353.5 2.0 fusion.50
  355.6 11.0 %all-to-all-done.4 = f32[1,8,4,20480]{3,1,0,2:T(8,128)S(1)} async-done(((f32[1,8,4,20480]{3,1,0,2:T(8,128)}), f32[1,8,4,20480]{3,1,0,2:T(8,128)S(1)}, u32[]{:S(2)}, u32[]{:S(2)}) %all-to-all-start.4) | async-done | bytes 2621472 | tf_op jit(solution)/shard_map/all_to_all | solution.py:250
  366.6 4.2 all-to-all-start.2
  370.7 1.5 fusion.73
  372.3 1.6 copy.64
  373.9 2.0 fusion.48
  375.9 5.2 all-to-all-done.2
  381.1 4.2 all-to-all-start.3
  385.2 4.3 fusion.96
  389.5 6.5 reshape.374
  396.0 7.9 copy.71
  403.9 5.1 all-to-all-start.7
  409.0 1.9 fusion.94
  410.9 2.6 copy.68
  413.5 54.9 %all-to-all-done.7 = f32[1,8,4,40960]{3,1,0,2:T(8,128)} async-done(((f32[1,8,4,40960]{3,1,0,2:T(8,128)}), f32[1,8,4,40960]{3,1,0,2:T(8,128)}, u32[]{:S(2)}, u32[]{:S(2)}) %all-to-all-start.7) | async-done | bytes 5242912 | tf_op jit(solution)/shard_map/all_to_all | solution.py:253
  468.4 5.1 all-to-all-start.5
  473.6 2.3 convolution_multiply_fusion
  478.3 4.0 reduce_sum.287
  482.9 2.1 fusion.44
  484.9 48.0 %all-to-all-done.5 = f32[640,8,4,64]{0,3,1,2:T(8,128)} async-done(((f32[640,8,4,64]{0,3,1,2:T(8,128)}), f32[640,8,4,64]{0,3,1,2:T(8,128)}, u32[]{:S(2)}, u32[]{:S(2)}) %all-to-all-start.5) | async-done | bytes 5242912 | tf_op jit(solution)/shard_map/all_to_all | solution.py:251
  533.0 3.7 all-to-all-start.1
  536.7 1.8 reduce_sum.281
  538.9 1.8 reduce_sum.282
  540.7 1.9 fusion.95
  542.7 2.7 copy.70
  545.3 22.6 %all-to-all-done.1 = f32[640,8,4,32]{0,3,1,2:T(8,128)S(1)} async-done(((f32[640,8,4,32]{0,3,1,2:T(8,128)}), f32[640,8,4,32]{0,3,1,2:T(8,128)S(1)}, u32[]{:S(2)}, u32[]{:S(2)}) %all-to-all-start.1) | async-done | bytes 2621472 | tf_op jit(solution)/shard_map/all_to_all | solution.py:246
  567.9 5.1 all-to-all-start.6
  574.2 4.0 reduce_sum.285
  578.3 54.2 %all-to-all-done.6 = f32[640,8,4,64]{0,3,1,2:T(8,128)} async-done(((f32[640,8,4,64]{0,3,1,2:T(8,128)}), f32[640,8,4,64]{0,3,1,2:T(8,128)}, u32[]{:S(2)}, u32[]{:S(2)}) %all-to-all-start.6) | async-done | bytes 5242912 | tf_op jit(solution)/shard_map/all_to_all | solution.py:252
  632.5 4.0 reduce_sum.286
  639.9 3.3 all-to-all-start
  644.0 3.0 all-to-all-done
  647.0 20.0 %all-reduce.1 = f32[1,8,96]{2,1,0:T(8,128)S(1)} all-reduce(f32[1,8,96]{2,1,0:T(8,128)S(1)} %bitcast.184), channel_id=4, replica_groups=mesh['dp'=8,'ctx'=4] {'dp'}, use_global_device_ids=true, to_apply=%region_23.24.clone | all-reduce | flops 768 | bytes 6144
  668.2 2.0 dynamic-slice_reduce_fusion.1
  670.8 2.4 dynamic-slice_reduce_fusion
  673.9 22.1 %reduce-scatter.24.cloned.1.call-done = f32[640,1,8]{0,2,1:T(8,128)} async-done(((f32[640,8,8]{0,2,1:T(8,128)}), f32[640,1,8]{0,2,1:T(8,128)}) %reduce-scatter.24.cloned.1.call-update) | async-done | bytes 20496
  696.0 64.8 %reduce-scatter.16.cloned.1.call-done = f32[640,1,32]{0,2,1:T(8,128)} async-done(((f32[640,8,32]{0,2,1:T(8,128)}), f32[640,1,32]{0,2,1:T(8,128)}) %reduce-scatter.16.cloned.1.call-update) | async-done | bytes 81936 | tf_op jit(solution)/shard_map/reduce_scatter | solution.py:257
  760.9 67.8 %reduce-scatter.18.cloned.1.call-done = f32[640,1,64]{0,2,1:T(8,128)} async-done(((f32[640,8,64]{0,2,1:T(8,128)}), f32[640,1,64]{0,2,1:T(8,128)}) %reduce-scatter.18.cloned.1.call-update) | async-done | bytes 163856 | tf_op jit(solution)/shard_map/reduce_scatter | solution.py:262
  828.6 67.5 %reduce-scatter.20.cloned.1.call-done = f32[640,1,64]{0,2,1:T(8,128)} async-done(((f32[640,8,64]{0,2,1:T(8,128)}), f32[640,1,64]{0,2,1:T(8,128)}) %reduce-scatter.20.cloned.1.call-update) | async-done | bytes 163856 | tf_op jit(solution)/shard_map/reduce_scatter | solution.py:263
  (196 shorter events, 33.2 us)
Async XLA Ops:
  7.2 142.3 %copy-start.3 = (bf16[1,128,640]{2,1,0:T(8,128)(2,1)S(1)}, bf16[1,128,640]{2,1,0:T(8,128)(2,1)}, u32[]{:S(2)}) copy-start(bf16[1,128,640]{2,1,0:T(8,128)(2,1)} %param.11) | copy-start | bytes 491524
  7.2 149.7 %copy-start.44 = (s32[1,128]{1,0:T(1,128)S(1)}, s32[1,128]{1,0:T(1,128)}, u32[]{:S(2)}) copy-start(s32[1,128]{1,0:T(1,128)} %param.13) | copy-start | bytes 1540
  7.2 149.8 %all-gather.7.cloned.1.call-start = ((), (), s32[]{:S(2)}) async-start(), calls=%async_computation.14 | async-start | bytes 1351680 | tf_op jit(solution)/shard_map/all_gather | solution.py:93
  7.9 155.6 %all-gather.9.cloned.1.call-start = ((), (), s32[]{:S(2)}) async-start(), calls=%async_computation.15 | async-start | bytes 1351680 | tf_op jit(solution)/shard_map/all_gather | solution.py:96
  8.7 175.7 %all-gather.11.cloned.1.call-start = ((), (), s32[]{:S(2)}) async-start(), calls=%async_computation.16 | async-start | bytes 2703360 | tf_op jit(solution)/shard_map/all_gather | solution.py:97
  9.4 234.6 %all-gather.13.cloned.1.call-start = ((), (), s32[]{:S(2)}) async-start(), calls=%async_computation.17 | async-start | bytes 2703360 | tf_op jit(solution)/shard_map/all_gather | solution.py:98
  10.0 293.7 %all-gather.15.cloned.1.call-start = ((), (), s32[]{:S(2)}) async-start(), calls=%async_computation.18 | async-start | bytes 2703360 | tf_op jit(solution)/shard_map/all_gather | solution.py:99
  10.6 336.3 %reduce-scatter.14.cloned.1.call-start = ((), (), s32[]{:S(2)}) async-start(), calls=%async_computation.19 | async-start | bytes 1310720 | tf_op jit(solution)/shard_map/reduce_scatter | solution.py:214
  53.6 106.0 %copy-start.35 = (f32[256]{0:T(256)}, f32[256]{0:T(256)S(1)}, u32[]{:S(2)}) copy-start(f32[256]{0:T(256)S(1)} %get-tuple-element.44) | copy-start | bytes 3076
  53.7 105.3 %copy-start.42 = (f32[128]{0:T(128)}, f32[128]{0:T(128)S(1)}, u32[]{:S(2)}) copy-start(f32[128]{0:T(128)S(1)} %negate_power_fusion) | copy-start | bytes 1540
  55.3 103.7 %copy-start.38 = (f32[128]{0:T(128)}, f32[128]{0:T(128)S(1)}, u32[]{:S(2)}) copy-start(f32[128]{0:T(128)S(1)} %get-tuple-element.51) | copy-start | bytes 1540
  96.7 0.7 copy-start.17
  98.7 61.0 %copy-start.21 = (f32[128,256]{1,0:T(8,128)}, f32[128,256]{1,0:T(8,128)S(1)}, u32[]{:S(2)}) copy-start(f32[128,256]{1,0:T(8,128)S(1)} %get-tuple-element.63) | copy-start | bytes 393220
  99.3 57.7 %copy-start.40 = (f32[128]{0:T(128)}, f32[128]{0:T(128)S(1)}, u32[]{:S(2)}) copy-start(f32[128]{0:T(128)S(1)} %get-tuple-element.53) | copy-start | bytes 1540
  99.3 60.5 %copy-start.43 = (f32[128]{0:T(128)}, f32[128]{0:T(128)S(1)}, u32[]{:S(2)}) copy-start(f32[128]{0:T(128)S(1)} %fusion.77) | copy-start | bytes 1540
  110.7 49.2 %copy-start.24 = (bf16[512,256]{1,0:T(8,128)(2,1)}, bf16[512,256]{1,0:T(8,128)(2,1)S(1)}, u32[]{:S(2)}) copy-start(bf16[512,256]{1,0:T(8,128)(2,1)S(1)} %all_gather.46) | copy-start | bytes 786436
  156.9 4.4 copy-start.31
  161.0 2.5 copy-start.25
  163.5 24.6 %copy-start.10 = (bf16[4,128,256]{1,2,0:T(8,128)(2,1)}, bf16[4,128,256]{1,2,0:T(8,128)(2,1)S(1)}, u32[]{:S(2)}) copy-start(bf16[4,128,256]{1,2,0:T(8,128)(2,1)S(1)} %copy.54) | copy-start | bytes 786436
  248.0 60.7 %copy-start.2 = (bf16[128,2048]{1,0:T(8,128)(2,1)}, bf16[128,2048]{1,0:T(8,128)(2,1)S(1)}, u32[]{:S(2)}) copy-start(bf16[128,2048]{1,0:T(8,128)(2,1)S(1)} %get-tuple-element.70) | copy-start | bytes 1572868
  248.0 58.3 %copy-start.15 = (bf16[1,128,640]{2,1,0:T(8,128)(2,1)S(1)}, bf16[1,128,640]{2,1,0:T(8,128)(2,1)}, u32[]{:S(2)}) copy-start(bf16[1,128,640]{2,1,0:T(8,128)(2,1)} %param.12) | copy-start | bytes 491524
  303.7 3.6 copy-start.6
  303.7 3.6 copy-start.9
  303.7 3.6 copy-start.27
  307.3 1.4 copy-start.28
  307.3 1.8 copy-start
  308.7 1.0 copy-start.13
  308.7 3.4 copy-start.12
  308.8 2.2 copy-start.1
  309.7 2.4 copy-start.16
  311.0 2.2 copy-start.4
  312.2 1.6 copy-start.30
  312.2 1.8 copy-start.26
  313.0 1.4 copy-start.7
  313.2 1.2 copy-start.14
  313.2 1.2 copy-start.32
  313.9 1.8 copy-start.23
  314.9 0.8 copy-start.11
  326.0 40.6 %all-to-all-start.4 = ((f32[1,8,4,20480]{3,1,0,2:T(8,128)}), f32[1,8,4,20480]{3,1,0,2:T(8,128)S(1)}, u32[]{:S(2)}, u32[]{:S(2)}) async-start(f32[1,8,4,20480]{3,1,0,2:T(8,128)} %copy.66), calls=%async_computation.6 | async-start | bytes 5242880 | tf_op jit(solution)/shard_map/all_to_all | solution.py:250
  366.6 14.5 %all-to-all-start.2 = ((f32[640,8,4,8]{0,3,1,2:T(8,128)}), f32[640,8,4,8]{0,3,1,2:T(8,128)}, u32[]{:S(2)}, u32[]{:S(2)}) async-start(f32[640,8,4,8]{0,3,1,2:T(8,128)} %fusion.50), calls=%async_computation.4 | async-start | bytes 1310720 | tf_op jit(solution)/shard_map/all_to_all | solution.py:247
  381.1 22.8 %all-to-all-start.3 = ((f32[640,8,4,8]{0,3,1,2:T(8,128)}), f32[640,8,4,8]{0,3,1,2:T(8,128)}, u32[]{:S(2)}, u32[]{:S(2)}) async-start(f32[640,8,4,8]{0,3,1,2:T(8,128)} %fusion.48), calls=%async_computation.5 | async-start | bytes 1310720 | tf_op jit(solution)/shard_map/all_to_all | solution.py:248
  403.9 64.5 %all-to-all-start.7 = ((f32[1,8,4,40960]{3,1,0,2:T(8,128)}), f32[1,8,4,40960]{3,1,0,2:T(8,128)}, u32[]{:S(2)}, u32[]{:S(2)}) async-start(f32[1,8,4,40960]{3,1,0,2:T(8,128)} %copy.71), calls=%async_computation.11 | async-start | bytes 10485760 | tf_op jit(solution)/shard_map/all_to_all | solution.py:253
  468.4 64.6 %all-to-all-start.5 = ((f32[640,8,4,64]{0,3,1,2:T(8,128)}), f32[640,8,4,64]{0,3,1,2:T(8,128)}, u32[]{:S(2)}, u32[]{:S(2)}) async-start(f32[640,8,4,64]{0,3,1,2:T(8,128)} %copy.68), calls=%async_computation.7 | async-start | bytes 10485760 | tf_op jit(solution)/shard_map/all_to_all | solution.py:251
  473.5 4.5 copy-start.36
  473.5 194.7 %all-reduce.9.cloned.1.call-start = ((), (), s32[]{:S(2)}) async-start(), calls=%async_computation.25 | async-start | bytes 3932160
  478.3 4.0 copy-start.37
  533.0 35.0 %all-to-all-start.1 = ((f32[640,8,4,32]{0,3,1,2:T(8,128)}), f32[640,8,4,32]{0,3,1,2:T(8,128)S(1)}, u32[]{:S(2)}, u32[]{:S(2)}) async-start(f32[640,8,4,32]{0,3,1,2:T(8,128)} %fusion.44), calls=%async_computation.2 | async-start | bytes 5242880 | tf_op jit(solution)/shard_map/all_to_all | solution.py:246
  536.7 137.2 %reduce-scatter.22.cloned.1.call-start = ((), (), s32[]{:S(2)}) async-start(), calls=%async_computation.23 | async-start | bytes 184320
  538.6 157.5 %reduce-scatter.24.cloned.1.call-start = ((), (), s32[]{:S(2)}) async-start(), calls=%async_computation.24 | async-start | bytes 184320
  567.9 64.5 %all-to-all-start.6 = ((f32[640,8,4,64]{0,3,1,2:T(8,128)}), f32[640,8,4,64]{0,3,1,2:T(8,128)}, u32[]{:S(2)}, u32[]{:S(2)}) async-start(f32[640,8,4,64]{0,3,1,2:T(8,128)} %copy.70), calls=%async_computation.9 | async-start | bytes 10485760 | tf_op jit(solution)/shard_map/all_to_all | solution.py:252
  573.0 187.9 %reduce-scatter.16.cloned.1.call-start = ((), (), s32[]{:S(2)}) async-start(), calls=%async_computation.20 | async-start | bytes 737280 | tf_op jit(solution)/shard_map/reduce_scatter | solution.py:257
  574.1 254.5 %reduce-scatter.18.cloned.1.call-start = ((), (), s32[]{:S(2)}) async-start(), calls=%async_computation.21 | async-start | bytes 1474560 | tf_op jit(solution)/shard_map/reduce_scatter | solution.py:262
  578.2 58.4 %copy-start.46 = (u32[32]{0:T(128)S(1)}, u32[32]{0:T(128)}, u32[]{:S(2)}) copy-start(u32[32]{0:T(128)} %constant.64) | copy-start | bytes 388
  578.2 59.0 %copy-start.5 = (bf16[640,1024]{0,1:T(8,128)(2,1)S(1)}, bf16[640,1024]{0,1:T(8,128)(2,1)}, u32[]{:S(2)}) copy-start(bf16[640,1024]{0,1:T(8,128)(2,1)} %all-gather.7.cloned.1.call-done) | copy-start | bytes 3932164
  578.2 317.9 %reduce-scatter.20.cloned.1.call-start = ((), (), s32[]{:S(2)}) async-start(), calls=%async_computation.22 | async-start | bytes 1474560 | tf_op jit(solution)/shard_map/reduce_scatter | solution.py:263
  636.5 1.1 copy-start.18
  636.5 1.1 copy-start.29
  636.5 1.3 copy-start.20
  636.5 2.6 copy-start.34
  636.5 2.6 copy-start.33
  636.5 2.7 copy-start.41
  636.6 6.6 copy-start.8
  636.6 6.6 copy-start.45
  639.9 7.1 all-to-all-start
  (3 other events, 2.0 us)
Sparse Core Ops, SparseCore 0:
  10.9 57.3 all-gather.6
  71.1 53.2 all-gather.8
  127.3 57.0 all-gather.10
  187.1 56.8 all-gather.12
  246.8 56.8 all-gather.14
  317.4 29.4 reduce-scatter.13
  482.4 98.6 all-reduce.8
  584.8 53.9 reduce-scatter.21
  642.6 53.4 reduce-scatter.23
  699.7 61.0 reduce-scatter.15
  765.2 63.3 reduce-scatter.17
  832.8 63.2 reduce-scatter.19
where the time goes:
time: 905 us; the launch traced here: 903 us
  waiting for transfers between devices  572 us (63%)
  blocking collectives  160 us (18%)
  local copies, waits for them, and re-layouts  45.8 us (5%)
  matrix products  42.8 us (5%)
  starting transfers between devices  34.9 us (4%)
  other arithmetic  32.7 us (4%)
  between operations  15.1 us (2%)
    reduce_scatter x1, waiting for transfers between devices, body(): lax.psum_scatter(local[5], 'dp', scatter_dimension=1, tiled=True)  67.8 us
    reduce_scatter x1, waiting for transfers between devices, body(): lax.psum_scatter(local[6], 'dp', scatter_dimension=1, tiled=True)  67.5 us
    reduce_scatter x1, waiting for transfers between devices, body(): lax.psum_scatter(local[0], 'dp', scatter_dimension=1, tiled=True)  64.8 us
    unnamed x2, blocking collectives  62.1 us
    all_gather x1, waiting for transfers between devices, body(): lax.all_gather(shards[5], ('dp', 'ctx'), axis=1, tiled=True)  56 us
    all_gather x1, waiting for transfers between devices, body(): lax.all_gather(shards[6], ('dp', 'ctx'), axis=0, tiled=True)  55.7 us
    all_to_all x1, waiting for transfers between devices, body(): lax.all_to_all(blocks[7], 'ctx', split_axis=2, concat_axis=2, tiled=True)  54.9 us
    all_to_all x1, waiting for transfers between devices, body(): lax.all_to_all(blocks[6], 'ctx', split_axis=2, concat_axis=2, tiled=True)  54.2 us
  transfers between devices with their start and end apart: 20, of which 15 were waited for; matrix products, arithmetic and copies ran while one was open for 12% of the time, Pallas kernels for 0%

commit v1 on v0

v1 whole, which is shorter than its diff:
```python
import functools

import jax
import jax.numpy as jnp
from jax import lax
from jax.experimental import pallas as pl
from jax.experimental.pallas import tpu as pltpu
from jax.sharding import PartitionSpec as P

D = 640
H = 4
HD = 256

EPS = 1e-06
ROPE_BASE = 1000000.0
NEGATIVE = -1e30
MESH = pl.DeviceIdType.MESH
BF = jnp.bfloat16
F32 = jnp.float32


def norm_forward(value, gain):
    factor = lax.rsqrt(jnp.mean(value * value, axis=-1, keepdims=True) + EPS)
    return (value * factor * gain, factor)


def norm_backward(value, factor, gain, grad_out):
    scaled = grad_out * gain
    grad_in = factor * scaled - value * (factor * factor * factor) * jnp.mean(
        scaled * value, axis=-1, keepdims=True
    )
    grad_gain = jnp.sum((grad_out * value * factor).reshape(-1, value.shape[-1]), axis=0)
    return (grad_in, grad_gain)


def rotary_tables(positions, width):
    exponent = jnp.arange(0, width, 2, dtype=jnp.int32).astype(F32) / width
    freqs = jnp.power(F32(ROPE_BASE), -exponent)
    theta = positions.astype(F32)[:, None] * freqs[None, :]
    return (jnp.cos(theta), jnp.sin(theta))


def rotate(value, cosine, sine):
    half = value.shape[-1] // 2
    first = value[..., :half]
    second = value[..., half:]
    return jnp.concatenate(
        [first * cosine - second * sine, second * cosine + first * sine], axis=-1
    )


def product(left, right):
    return jnp.dot(left, right, preferred_element_type=F32)


def inner_rows(left, right):
    return lax.dot_general(left, right, (((0,), (0,)), ((), ())), preferred_element_type=F32)


def against(left, right):
    return lax.dot_general(left, right, (((1,), (1,)), ((), ())), preferred_element_type=F32)


def gelu_mix(gate_in, up_in):
    return jax.nn.gelu(gate_in, approximate=True) * up_in


Z = 4
ORDER = (0, 1, 3, 2)


def coordinates():
    dp = lax.axis_index("dp")
    ctx = lax.axis_index("ctx")
    return dp // 2, dp % 2, ctx // 2, ctx % 2


def slot(z, x, y, c):
    return (z * 2 + x) * 4 + y * 2 + c


def device(z, x, y, c):
    return (z * 2 + x, y * 2 + c)


def flip(bit, by):
    return 1 - bit if by else bit


def greet(peers):
    barrier = pltpu.get_barrier_semaphore()
    for peer in peers:
        pl.semaphore_signal(barrier, inc=1, device_id=peer, device_id_type=MESH)
    pl.semaphore_wait(barrier, len(peers))


def gather_kernel(cut, w_ref, t_ref, out, tout, send, recv, tsend, trecv, local):
    z, x, y, c = coordinates()
    rows = w_ref.shape[0]
    part = (pl.ds(0, cut), pl.ds(cut, rows - cut))
    to_z = {k: device((z + k) % Z, x, y, c) for k in (1, 2, 3)}
    to_x, to_y, to_c = device(z, 1 - x, y, c), device(z, x, 1 - y, c), device(z, x, y, 1 - c)
    to_d = device(z, x, 1 - y, 1 - c)
    greet([to_z[1], to_z[2], to_z[3], to_x, to_y, to_c, to_d])
    started = []

    def block(k, a, b, core):
        return slot((z + Z - k) % Z, flip(x, a), flip(y, b), core)

    def copy(index, source, target, peer, sends=send, recvs=recv):
        return pltpu.make_async_remote_copy(
            src_ref=source,
            dst_ref=target,
            send_sem=sends.at[index],
            recv_sem=recvs.at[index],
            device_id=peer,
            device_id_type=MESH,
        )

    def push(index, k, a, b, p, peer):
        where = block(k, a, b, c)
        source = w_ref.at[part[p]] if (k, a, b) == (0, 0, 0) else out.at[where, part[p]]
        one = copy(index, source, out.at[where, part[p]], peer)
        one.start()
        started.append(one)

    def arrived(index, k, a, b, p, core):
        where = out.at[block(k, a, b, core), part[p]]
        copy(index, where, where, to_c).wait_recv()

    def z_at(k, p):
        return (k - 1) * 2 + p

    def one_at(k, p):
        return 6 + k * 2 + p

    def two_at(k, j, p):
        return 14 + (k * 2 + j) * 2 + p

    def core_at(k, a, b, p):
        return 30 + ((k * 2 + a) * 2 + b) * 2 + p

    def sibling(k, a, b, p):
        push(core_at(k, a, b, p), k, a, b, p, to_c)

    def have_line(k):
        for p in range(2):
            push(one_at(k, p), k, 0, 0, p, (to_x, to_y)[p])
            push(two_at(k, 0, p), k, 0, 0, p, (to_y, to_x)[p])
        for p in range(2):
            sibling(k, 0, 0, p)

    mine = lax.axis_index("ctx")
    for i, peer in enumerate((to_c, to_y, to_d)):
        one = copy(i, t_ref, tout.at[mine], peer, tsend, trecv)
        one.start()
        started.append(one)
    keep = (
        pltpu.make_async_copy(t_ref, tout.at[mine], local.at[0]),
        pltpu.make_async_copy(w_ref, out.at[block(0, 0, 0, c)], local.at[1]),
    )
    for one in keep:
        one.start()
    for k in (1, 3, 2):
        for p in range(2):
            where = block(0, 0, 0, c)
            one = copy(z_at(k, p), w_ref.at[part[p]], out.at[where, part[p]], to_z[k])
            one.start()
            started.append(one)
    have_line(0)

    def have_one(k):
        for p in range(2):
            a, b = (1, 0) if p == 0 else (0, 1)
            arrived(one_at(k, p), k, a, b, p, c)
            push(two_at(k, 1, p), k, a, b, p, (to_y, to_x)[p])
            sibling(k, a, b, p)

    def have_two(k, j):
        for p in range(2):
            a, b = (j, 1) if p == 0 else (1, j)
            arrived(two_at(k, j, p), k, a, b, p, c)
            sibling(k, a, b, p)

    for step, k in enumerate(ORDER):
        if k:
            for p in range(2):
                arrived(z_at(k, p), k, 0, 0, p, c)
            have_line(k)
            have_one(ORDER[step - 1])
    have_one(ORDER[-1])
    for k in ORDER:
        have_two(k, 0)
    for k in ORDER:
        have_two(k, 1)
    for k in range(Z):
        for a in range(2):
            for b in range(2):
                for p in range(2):
                    arrived(core_at(k, a, b, p), k, a, b, p, 1 - c)
    for i, other in enumerate((y * 2 + 1 - c, (1 - y) * 2 + c, (1 - y) * 2 + 1 - c)):
        copy(i, t_ref, tout.at[other], to_c, tsend, trecv).wait_recv()
    for one in keep:
        one.wait()
    for one in started:
        one.wait_send()


def gather_call(packed, extra, devices, cycle):
    cut = packed.shape[0] // 32 * 16
    return pl.pallas_call(
        functools.partial(gather_kernel, cut),
        out_shape=(
            jax.ShapeDtypeStruct((devices,) + packed.shape, BF),
            jax.ShapeDtypeStruct((cycle,) + extra.shape, BF),
        ),
        in_specs=[pl.BlockSpec(memory_space=pl.ANY)] * 2,
        out_specs=[pl.BlockSpec(memory_space=pl.ANY)] * 2,
        scratch_shapes=[
            pltpu.SemaphoreType.DMA((62,)),
            pltpu.SemaphoreType.DMA((62,)),
            pltpu.SemaphoreType.DMA((3,)),
            pltpu.SemaphoreType.DMA((3,)),
            pltpu.SemaphoreType.DMA((2,)),
        ],
        compiler_params=pltpu.CompilerParams(collective_id=0, has_side_effects=True),
        name="gather_weights",
    )(packed, extra)


def reduce_kernel(cut, g_ref, out, cbuf, abuf, bbuf, zbuf, send, recv):
    z, x, y, c = coordinates()
    rows = g_ref.shape[1]
    part = (pl.ds(0, cut), pl.ds(cut, rows - cut))
    to_z = {k: device((z + k) % Z, x, y, c) for k in (1, 2, 3)}
    to_x, to_y, to_c = device(z, 1 - x, y, c), device(z, x, 1 - y, c), device(z, x, y, 1 - c)
    greet([to_z[1], to_z[2], to_z[3], to_x, to_y, to_c])
    started = []

    def push(index, source, target, peer):
        one = pltpu.make_async_remote_copy(
            src_ref=source,
            dst_ref=target,
            send_sem=send.at[index],
            recv_sem=recv.at[index],
            device_id=peer,
            device_id_type=MESH,
        )
        one.start()
        started.append(one)

    def arrived(index, target):
        pltpu.make_async_remote_copy(
            src_ref=target,
            dst_ref=target,
            send_sem=send.at[index],
            recv_sem=recv.at[index],
            device_id=to_c,
            device_id_type=MESH,
        ).wait_recv()

    def place(k, a, b):
        return (k * 2 + a) * 2 + b

    def block(k, a, b, core):
        return slot((z + k) % Z, flip(x, a), flip(y, b), core)

    far = [(k, a, b) for a, b in ((1, 1), (0, 1), (1, 0), (0, 0)) for k in (2, 1, 3, 0)]
    for k, a, b in far:
        i = place(k, a, b)
        push(i, g_ref.at[block(k, a, b, 1 - c)], cbuf.at[i], to_c)
    for k, a, b in far:
        i = place(k, a, b)
        arrived(i, cbuf.at[i])
        cbuf[i] = cbuf[i] + g_ref[block(k, a, b, c)]
        if b:
            j = k * 2 + a
            push(16 + j * 2, cbuf.at[i, part[0]], abuf.at[j, part[0]], to_y)
        if a:
            j = k * 2 + b
            push(17 + j * 2, cbuf.at[i, part[1]], abuf.at[j, part[1]], to_x)
    for near in (1, 0):
        for k in (2, 1, 3, 0):
            for p in range(2):
                j = k * 2 + near
                i = place(k, near, 0) if p == 0 else place(k, 0, near)
                arrived(16 + j * 2 + p, abuf.at[j, part[p]])
                abuf[j, part[p]] = abuf[j, part[p]] + cbuf[i, part[p]]
                if near:
                    push(
                        32 + k * 2 + p,
                        abuf.at[j, part[p]],
                        bbuf.at[k, part[p]],
                        (to_x, to_y)[p],
                    )
    for k in (2, 1, 3, 0):
        for p in range(2):
            arrived(32 + k * 2 + p, bbuf.at[k, part[p]])
            bbuf[k, part[p]] = bbuf[k, part[p]] + abuf[k * 2, part[p]]
            if k:
                push(
                    40 + (k - 1) * 2 + p,
                    bbuf.at[k, part[p]],
                    zbuf.at[k - 1, part[p]],
                    to_z[k],
                )
    out[...] = bbuf[0].astype(F32)
    for k in (1, 3, 2):
        for p in range(2):
            arrived(40 + (k - 1) * 2 + p, zbuf.at[k - 1, part[p]])
            out[part[p]] = out[part[p]] + zbuf[k - 1, part[p]].astype(F32)
    for one in started:
        one.wait_send()


def reduce_call(terms):
    shape = terms.shape[1:]
    cut = shape[0] // 32 * 16
    return pl.pallas_call(
        functools.partial(reduce_kernel, cut),
        out_shape=jax.ShapeDtypeStruct(shape, F32),
        in_specs=[pl.BlockSpec(memory_space=pltpu.VMEM)],
        out_specs=pl.BlockSpec(memory_space=pltpu.VMEM),
        scratch_shapes=[
            pltpu.VMEM((16,) + shape, BF),
            pltpu.VMEM((8,) + shape, BF),
            pltpu.VMEM((4,) + shape, BF),
            pltpu.VMEM((3,) + shape, BF),
            pltpu.SemaphoreType.DMA((46,)),
            pltpu.SemaphoreType.DMA((46,)),
        ],
        compiler_params=pltpu.CompilerParams(
            collective_id=1, has_side_effects=True, vmem_limit_bytes=48 * 1024 * 1024
        ),
        name="reduce_gradients",
    )(terms)


def exchange_kernel(g_ref, out, buf, send, recv):
    z, x, y, c = coordinates()
    others = ((y, 1 - c), (1 - y, c), (1 - y, 1 - c))
    greet([device(z, x, *other) for other in others])
    started = []
    for i in (2, 1, 0):
        yy, cc = others[i]
        one = pltpu.make_async_remote_copy(
            src_ref=g_ref.at[yy * 2 + cc],
            dst_ref=buf.at[i],
            send_sem=send.at[i],
            recv_sem=recv.at[i],
            device_id=device(z, x, yy, cc),
            device_id_type=MESH,
        )
        one.start()
        started.append(one)
    out[...] = g_ref[y * 2 + c].astype(F32)
    for one, i in zip(started[::-1], range(3)):
        one.wait_recv()
        out[...] = out[...] + buf[i].astype(F32)
    for one in started:
        one.wait_send()


def exchange_call(terms):
    shape = terms.shape[1:]
    return pl.pallas_call(
        exchange_kernel,
        out_shape=jax.ShapeDtypeStruct(shape, F32),
        in_specs=[pl.BlockSpec(memory_space=pltpu.VMEM)],
        out_specs=pl.BlockSpec(memory_space=pltpu.VMEM),
        scratch_shapes=[
            pltpu.VMEM((3,) + shape, BF),
            pltpu.SemaphoreType.DMA((3,)),
            pltpu.SemaphoreType.DMA((3,)),
        ],
        compiler_params=pltpu.CompilerParams(
            collective_id=2, has_side_effects=True, vmem_limit_bytes=16 * 1024 * 1024
        ),
        name="exchange_keys",
    )(terms)


def body(
    kernels, tokens, cotangent, segments, gains, w_query, w_key, w_value, w_out, w_gate, w_up, w_down
):
    resid = tokens[0].astype(F32)
    rows = resid.shape[0]
    cycle = lax.axis_size("ctx")
    groups = lax.axis_size("dp")
    devices = cycle * groups
    place = lax.axis_index("ctx")
    scale = HD ** (-0.5)
    doc_local = segments[0]
    own = (w_query.T, w_key.T, w_value.T, w_out, w_gate.T, w_up.T, w_down)
    own += (jnp.pad(gains[None], ((0, 0), (0, D - gains.shape[0]))),)
    counts = [piece.shape[0] for piece in own]
    starts = [sum(counts[:i]) for i in range(len(counts))]
    height = -(-sum(counts) // 16) * 16 if kernels else sum(counts)
    packed = jnp.pad(jnp.concatenate(own, axis=0), ((0, height - sum(counts)), (0, 0)))
    if kernels:
        marks = jnp.pad(doc_local.astype(BF)[None], ((0, 15), (0, D - rows)))
        every, near = gather_call(
            packed, jnp.concatenate([tokens[0], marks], axis=0), devices, cycle
        )
        tokens_all = near[:, :rows].reshape(cycle * rows, D)
        doc_all = near[:, rows, :rows].reshape(cycle * rows).astype(jnp.int32)
    else:
        every = lax.all_gather(packed, ("dp", "ctx"), axis=0, tiled=False)
        tokens_all = lax.all_gather(tokens[0], "ctx", axis=0, tiled=True)
        doc_all = lax.all_gather(doc_local, "ctx", axis=0, tiled=True)
    wq, wk, wv, wo, wg, wu, wd = [
        every[:, s : s + n].reshape(devices * n, D) for s, n in zip(starts[:7], counts[:7])
    ]
    gain_all = every[:, starts[7], : gains.shape[0]].reshape(-1).astype(F32)
    g_in = gain_all[0:D]
    g_post_attn = gain_all[D : 2 * D]
    g_pre_ff = gain_all[2 * D : 3 * D]
    g_post_ff = gain_all[3 * D : 4 * D]
    g_query = gain_all[4 * D : 4 * D + HD]
    g_key = gain_all[4 * D + HD : 4 * D + 2 * HD]

    normed_f, in_factor = norm_forward(resid, g_in)
    normed = normed_f.astype(BF)
    normed_all = norm_forward(tokens_all.astype(F32), g_in)[0].astype(BF)
    queries = against(normed, wq).reshape(rows, H, HD)
    keys_all = against(normed_all, wk)
    values_all = against(normed_all, wv).astype(BF)
    positions = place * rows + jnp.arange(rows, dtype=jnp.int32)
    cos_all, sin_all = rotary_tables(jnp.arange(cycle * rows, dtype=jnp.int32), HD)
    cosine = lax.dynamic_slice_in_dim(cos_all, place * rows, rows, 0)
    sine = lax.dynamic_slice_in_dim(sin_all, place * rows, rows, 0)
    query_normed, query_factor = norm_forward(queries, g_query)
    key_normed, key_factor_all = norm_forward(keys_all, g_key)
    keys = lax.dynamic_slice_in_dim(keys_all, place * rows, rows, 0)
    key_factor = lax.dynamic_slice_in_dim(key_factor_all, place * rows, rows, 0)
    query_rot = (rotate(query_normed, cosine[:, None, :], sine[:, None, :]) * scale).astype(BF)
    key_rot = rotate(key_normed, cos_all, sin_all).astype(BF)
    query_rows = jnp.transpose(query_rot, (1, 0, 2)).reshape(H * rows, HD)
    query_pos = jnp.tile(positions, H)
    query_doc = jnp.tile(doc_local, H)
    key_pos = jnp.arange(cycle * rows, dtype=jnp.int32)
    allowed = (key_pos[None, :] <= query_pos[:, None]) & (doc_all[None, :] == query_doc[:, None])
    masked = jnp.where(allowed, against(query_rows, key_rot), NEGATIVE)
    top = jnp.max(masked, axis=1, keepdims=True)
    weights = jnp.where(allowed, jnp.exp(masked - top), 0.0)
    probs = weights / jnp.sum(weights, axis=1, keepdims=True)
    probs_low = probs.astype(BF)
    probs_rest = (probs - probs_low.astype(F32)).astype(BF)
    attended_rows = product(probs_low, values_all) + product(probs_rest, values_all)
    attended = jnp.transpose(attended_rows.reshape(H, rows, HD), (1, 0, 2))
    heads = attended.reshape(rows, H * HD).astype(BF)
    branch = product(heads, wo)
    attn_normed, branch_factor = norm_forward(branch, g_post_attn)
    hidden = resid + attn_normed
    ff_f, ff_factor = norm_forward(hidden, g_pre_ff)
    ff_in = ff_f.astype(BF)
    gate = against(ff_in, wg)
    up_proj = against(ff_in, wu)
    mid = gelu_mix(gate, up_proj).astype(BF)
    down = product(mid, wd)
    down_normed, down_factor = norm_forward(down, g_post_ff)
    mixed = (hidden + down_normed).astype(BF)

    grad_out = cotangent[0].astype(F32)
    grad_down_f, grad_g_post_ff = norm_backward(down, down_factor, g_post_ff, grad_out)
    grad_down = grad_down_f.astype(BF)
    w_down_part = inner_rows(mid, grad_down)
    grad_mid = against(grad_down, wd)
    _, gelu_back = jax.vjp(gelu_mix, gate, up_proj)
    grad_gate_f, grad_up_f = gelu_back(grad_mid)
    grad_gate = grad_gate_f.astype(BF)
    grad_up = grad_up_f.astype(BF)
    w_gate_part = inner_rows(grad_gate, ff_in)
    w_up_part = inner_rows(grad_up, ff_in)
    grad_ff = product(grad_gate, wg) + product(grad_up, wu)
    hidden_part, grad_g_pre_ff = norm_backward(hidden, ff_factor, g_pre_ff, grad_ff)
    grad_hidden = grad_out + hidden_part
    grad_branch_f, grad_g_post_attn = norm_backward(branch, branch_factor, g_post_attn, grad_hidden)
    grad_branch = grad_branch_f.astype(BF)
    w_out_part = inner_rows(heads, grad_branch)
    grad_att = against(grad_branch, wo).reshape(rows, H, HD).astype(BF)
    grad_rows = jnp.transpose(grad_att, (1, 0, 2)).reshape(H * rows, HD)
    delta = jnp.sum(grad_rows.astype(F32) * attended_rows, axis=1, keepdims=True)
    grad_probs = against(grad_rows, values_all)
    grad_logits = (probs * (grad_probs - delta)).astype(BF)
    grad_qrows = product(grad_logits, key_rot)
    grad_key_part = inner_rows(grad_logits, query_rows)
    grad_value_part = inner_rows(probs_low, grad_rows)
    grad_kv = jnp.concatenate([grad_key_part, grad_value_part], axis=1)
    if kernels:
        key_grad = exchange_call(grad_kv.astype(BF).reshape(cycle, rows, 2 * HD))
    else:
        key_grad = lax.psum_scatter(grad_kv, "ctx", scatter_dimension=0, tiled=True)
    grad_krot = key_grad[:, :HD]
    grad_values = key_grad[:, HD:].astype(BF)
    grad_qrot = jnp.transpose(grad_qrows.reshape(H, rows, HD), (1, 0, 2))
    grad_qn = rotate(grad_qrot * scale, cosine[:, None, :], -sine[:, None, :])
    grad_queries_f, grad_g_query = norm_backward(queries, query_factor, g_query, grad_qn)
    grad_queries = grad_queries_f.reshape(rows, H * HD).astype(BF)
    grad_kn = rotate(grad_krot, cosine, -sine)
    grad_keys_f, grad_g_key = norm_backward(keys, key_factor, g_key, grad_kn)
    grad_keys = grad_keys_f.astype(BF)
    w_query_part = inner_rows(grad_queries, normed)
    w_key_part = inner_rows(grad_keys, normed)
    w_value_part = inner_rows(grad_values, normed)
    grad_normed = product(grad_queries, wq) + product(grad_keys, wk) + product(grad_values, wv)
    input_part, grad_g_in = norm_backward(resid, in_factor, g_in, grad_normed)
    tokens_grad = (grad_hidden + input_part).astype(BF)
    gains_part = jnp.concatenate(
        [grad_g_in, grad_g_post_attn, grad_g_pre_ff, grad_g_post_ff, grad_g_query, grad_g_key]
    ).reshape(devices, 1, -1)
    terms = [
        part.reshape(devices, -1, D)
        for part in (
            w_query_part,
            w_key_part,
            w_value_part,
            w_out_part,
            w_gate_part,
            w_up_part,
            w_down_part,
        )
    ]
    tail = ((0, 0), (0, height - sum(counts)), (0, D - gains.shape[0]))
    terms.append(jnp.pad(gains_part, tail))
    kind = BF if kernels else F32
    stacked = jnp.concatenate([term.astype(kind) for term in terms], axis=1)
    if kernels:
        owned = reduce_call(stacked)
    else:
        owned = lax.psum_scatter(stacked, ("dp", "ctx"), scatter_dimension=0, tiled=False)
    q, k, v, o, g, u, d, s = [owned[a : a + n] for a, n in zip(starts, counts)]
    return (
        mixed[None],
        tokens_grad[None],
        s[0, : gains.shape[0]],
        q.T,
        k.T,
        v.T,
        o,
        g.T,
        u.T,
        d,
    )


def solution(mesh):
    kernels = (mesh.shape["dp"], mesh.shape["ctx"]) == (8, 4)
    return jax.shard_map(
        functools.partial(body, kernels),
        mesh=mesh,
        in_specs=(
            P("dp", "ctx", None),
            P("dp", "ctx", None),
            P("dp", "ctx"),
            P(("dp", "ctx")),
            P(None, ("dp", "ctx")),
            P(None, ("dp", "ctx")),
            P(None, ("dp", "ctx")),
            P(("dp", "ctx"), None),
            P(None, ("dp", "ctx")),
            P(None, ("dp", "ctx")),
            P(("dp", "ctx"), None),
        ),
        out_specs=(
            P("dp", "ctx", None),
            P("dp", "ctx", None),
            P(("dp", "ctx")),
            P(None, ("dp", "ctx")),
            P(None, ("dp", "ctx")),
            P(None, ("dp", "ctx")),
            P(("dp", "ctx"), None),
            P(None, ("dp", "ctx")),
            P(None, ("dp", "ctx")),
            P(("dp", "ctx"), None),
        ),
        check_vma=False,
    )
```

time: 905 us -> 239 us (0.26)
  waiting for transfers between devices: 572 us -> 0 us
  blocking collectives: 160 us -> 0 us
  Pallas kernels: 0 us -> 152 us
  starting transfers between devices: 34.9 us -> 0 us
  local copies, waits for them, and re-layouts: 45.8 us -> 30.9 us
  between operations: 15.1 us -> 1.86 us
  other arithmetic: 32.7 us -> 20.8 us
  matrix products: 42.8 us -> 31.8 us
    reduce_scatter x4 -> x0, waiting for transfers between devices: 217 us -> none  [the longest x1 67.8 us: body(): lax.psum_scatter(local[5], 'dp', scatter_dimension=1, tiled=True)]
    all_to_all x8 -> x0, waiting for transfers between devices: 199 us -> none  [the longest x1 54.9 us: body(): lax.all_to_all(blocks[7], 'ctx', split_axis=2, concat_axis=2, tiled=True)]
    pallas_call x0 -> x3, Pallas kernels: none -> 152 us  [the longest x1 77.9 us: reduce_call(): pl.pallas_call(functools.partial(reduce_kernel, cut), out_shape=jax.Shape...]
    all_gather x5 -> x0, waiting for transfers between devices: 130 us -> none  [the longest x1 56 us: body(): lax.all_gather(shards[5], ('dp', 'ctx'), axis=1, tiled=True)]
    all_gather x5 -> x0, blocking collectives: 97.6 us -> none  [the longest x1 41.4 us: body(): lax.all_gather(shards[1], ('dp', 'ctx'), axis=1, tiled=True)]
    unnamed x2 -> x0, blocking collectives: 62.1 us -> none
    all_to_all x8 -> x0, starting transfers between devices: 34.1 us -> none  [the longest x1 5.09 us: body(): lax.all_to_all(blocks[5], 'ctx', split_axis=2, concat_axis=2, tiled=True)]
    reshape x11 -> x1, local copies, waits for them, and re-layouts: 30.1 us -> 0.09 us  [body(): gains_part = jnp.concatenate([grad_g_in, grad_g_post_attn, grad_g_pre_ff,...]
  transfers between devices with their start and end apart: 20 -> 0, of which waited for: 15 -> 0; matrix products, arithmetic and copies ran while one was open for 12% -> 0% of each run, Pallas kernels for 0% -> 0%
where the time goes in v1:
time: 239 us; the launch traced here: 238 us
  Pallas kernels  152 us (64%)
  matrix products  31.8 us (13%)
  local copies, waits for them, and re-layouts  30.9 us (13%)
  other arithmetic  20.8 us (9%)
    pallas_call x1, Pallas kernels, reduce_call(): pl.pallas_call(functools.partial(reduce_kernel, cut), out_shape=jax.Shape...  77.9 us
    pallas_call x1, Pallas kernels, gather_call(): pl.pallas_call(functools.partial(gather_kernel, cut), out_shape=(jax.Shap...  65.4 us
    unnamed x133, local copies, waits for them, and re-layouts  15.3 us
    dot_general x9, matrix products, against(): lax.dot_general(left, right, (((1,), (1,)), ((), ())), preferred_element_...  11.7 us
    dot_general x9, matrix products, inner_rows(): lax.dot_general(left, right, (((0,), (0,)), ((), ())), preferred_element_...  10.7 us
    dot_general x10, matrix products, product(): return jnp.dot(left, right, preferred_element_type=F32)  9.42 us
    pallas_call x1, Pallas kernels, exchange_call(): pl.pallas_call(exchange_kernel, out_shape=jax.ShapeDtypeStruct(shape, F32...  8.88 us
    slice x2, local copies, waits for them, and re-layouts, body(): every[:, s:s + n].reshape(devices * n, D)  5.96 us

profile of v1, /device:TPU:0, one launch (start us, length us, event | category | flops | bytes accessed | tf_op | source)
XLA Modules:
  0.0 237.5 jit_solution(17948562033922790427)
XLA Ops:
  0.6 0.8 bitcast_dynamic-update-slice_fusion.2
  1.4 0.7 constant_dynamic-update-slice_fusion.4
  2.1 0.7 constant_dynamic-update-slice_fusion.3
  2.8 0.8 constant_dynamic-update-slice_fusion.2
  3.6 0.9 bitcast_dynamic-update-slice_fusion.1
  4.5 0.9 bitcast_dynamic-update-slice_fusion
  5.4 0.9 constant_dynamic-update-slice_fusion.1
  6.4 0.7 constant_dynamic-update-slice_fusion
  7.0 0.8 pad.18.w_ref
  8.5 1.6 fusion.52.t_ref
  10.1 65.4 %gather_weights.1 = (bf16[32,288,640]{2,1,0:T(8,128)(2,1)}, bf16[4,144,640]{2,1,0:T(8,128)(2,1)}) custom-call(bf16[288,640]{1,0:T(8,128)(2,1)} %pad.18.w_ref, bf16[144,640]{1,0:T(8,128)(2,1)} %fusion.52.t_ref), custom_call_target="tpu_custom_call" | custom-call | tf_op jit(solution)/shard_map/gather_weights/pallas_call | solution.py:211
  75.5 0.9 convert_reduce_fusion
  76.5 1.3 fusion.2
  77.8 1.3 fusion.4
  79.1 0.9 copy-done.24
  80.0 2.1 convolution_convert_fusion.10
  82.1 0.7 slice_convert_fusion.2
  82.9 2.0 fusion.73
  86.8 0.9 multiply_multiply_fusion.4
  87.7 2.2 multiply_reduce_fusion.3
  89.9 2.1 copy.27
  92.0 1.2 multiply_multiply_fusion.3
  93.2 1.9 subtract_convert_fusion.4
  95.1 1.5 fusion.71
  96.6 1.1 multiply_subtract_fusion.1
  97.8 0.7 copy-done.18
  98.5 1.3 fusion.22
  101.0 1.6 fusion.78
  102.6 1.8 copy.28
  104.4 1.4 multiply_reduce_fusion.11
  106.2 4.0 %fusion.72 = (bf16[32,64,640]{2,1,0:T(8,128)(2,1)S(1)}, bf16[32,64,640]{2,1,0:T(8,128)(2,1)S(1)}, bf16[32,64,640]{2,1,0:T(8,128)(2,1)S(1)}) fusion(bf16[32,288,640]{2,1,0:T(8,128)(2,1)} %get-tuple-element.13), kind=kLoop, calls=%fused_computation.193 | loop fusion | bytes 15728640 | tf_op jit(solution)/shard_map/slice | solution.py:412
  110.2 0.9 fusion.79
  111.2 1.0 multiply_convert_fusion.2
  112.2 0.8 copy-done.1
  113.0 0.7 multiply_reduce_fusion.9
  113.7 0.7 fusion.31
  114.4 0.8 fusion.28
  115.2 1.4 multiply_convert_fusion.1
  117.2 0.7 multiply_reduce_fusion.5
  118.0 0.8 multiply_reduce_fusion.6
  120.4 1.6 fusion.14
  122.1 0.8 convolution_multiply_fusion
  123.0 0.7 multiply_reduce_fusion
  124.6 1.4 convolution_convert_fusion.7
  126.0 1.3 convolution_convert_fusion.8
  127.4 8.9 %exchange_keys.1 = f32[128,512]{1,0:T(8,128)S(1)} custom-call(bf16[4,128,512]{2,1,0:T(8,128)(2,1)S(1)} %pad_maximum_fusion.1.g_ref), custom_call_target="tpu_custom_call" | custom-call | tf_op jit(solution)/shard_map/exchange_keys/pallas_call | solution.py:366
  136.3 0.7 fusion.62
  137.4 1.2 convolution_add_fusion.2
  138.6 1.4 fusion.39
  140.0 0.8 fusion.58
  140.8 1.6 fusion.1
  142.6 1.1 fusion.6
  143.8 1.1 fusion.5
  144.9 1.6 fusion
  146.5 0.9 convolution_convert_fusion.2
  147.4 1.8 constant_dynamic-update-slice_fusion.7
  149.2 0.9 convolution_convert_fusion.1
  150.3 1.8 constant_dynamic-update-slice_fusion.6
  152.1 0.9 convolution_convert_fusion
  153.0 1.8 constant_dynamic-update-slice_fusion.5
  156.1 0.9 pad_dynamic-update-slice_fusion.g_ref
  157.1 77.9 %reduce_gradients.1 = f32[288,640]{1,0:T(8,128)S(1)} custom-call(bf16[32,288,640]{2,1,0:T(8,128)(2,1)} %pad_dynamic-update-slice_fusion.g_ref), custom_call_target="tpu_custom_call" | custom-call | tf_op jit(solution)/shard_map/reduce_gradients/pallas_call | solution.py:319
  235.5 0.7 fusion.75
  236.8 0.8 fusion.74
  (168 shorter events, 10.3 us)
Async XLA Ops:
  5.4 76.7 %copy-start.56 = (s32[1,128]{1,0:T(1,128)S(1)}, s32[1,128]{1,0:T(1,128)}, u32[]{:S(2)}) copy-start(s32[1,128]{1,0:T(1,128)} %param.13) | copy-start | bytes 1540
  79.1 0.9 copy-start.24
  82.1 18.9 %copy-start.42 = (s32[512]{0:T(512)}, s32[512]{0:T(512)S(1)}, u32[]{:S(2)}) copy-start(s32[512]{0:T(512)S(1)} %get-tuple-element.95) | copy-start | bytes 6148
  82.1 18.9 %copy-start.44 = (s32[512]{0:T(512)}, s32[512]{0:T(512)S(1)}, u32[]{:S(2)}) copy-start(s32[512]{0:T(512)S(1)} %get-tuple-element.96) | copy-start | bytes 6148
  82.9 18.2 %copy-start.46 = (s32[4,1,128]{2,1,0:T(1,128)}, s32[4,1,128]{2,1,0:T(1,128)S(1)}, u32[]{:S(2)}) copy-start(s32[4,1,128]{2,1,0:T(1,128)S(1)} %slice_convert_fusion.2) | copy-start | bytes 6148
  82.9 2.0 copy-start
  84.8 2.9 %copy-start.25 = (bf16[4,128,640]{2,1,0:T(8,128)(2,1)S(1)}, bf16[4,128,640]{2,1,0:T(8,128)(2,1)}, u32[]{:S(2)}) copy-start(bf16[4,128,640]{2,1,0:T(8,128)(2,1)} %copy-done.24) | copy-start | bytes 1966084
  85.5 0.7 copy-start.38
  86.2 8.9 %copy-start.34 = (f32[256]{0:T(256)}, f32[256]{0:T(256)S(1)}, u32[]{:S(2)}) copy-start(f32[256]{0:T(256)S(1)} %get-tuple-element.63) | copy-start | bytes 3076
  86.2 8.9 %copy-start.36 = (f32[256]{0:T(256)}, f32[256]{0:T(256)S(1)}, u32[]{:S(2)}) copy-start(f32[256]{0:T(256)S(1)} %get-tuple-element.64) | copy-start | bytes 3076
  86.8 8.3 %copy-start.32 = (f32[128,4]{0,1:T(4,128)}, f32[128,4]{0,1:T(4,128)S(1)}, u32[]{:S(2)}) copy-start(f32[128,4]{0,1:T(4,128)S(1)} %get-tuple-element.68) | copy-start | bytes 6148
  92.0 3.1 %copy-start.40 = (f32[512]{0:T(512)}, f32[512]{0:T(512)S(1)}, u32[]{:S(2)}) copy-start(f32[512]{0:T(512)S(1)} %add_rsqrt_fusion) | copy-start | bytes 6148
  96.6 3.6 %copy-start.26 = (f32[128,128]{1,0:T(8,128)}, f32[128,128]{1,0:T(8,128)S(1)}, u32[]{:S(2)}) copy-start(f32[128,128]{1,0:T(8,128)S(1)} %get-tuple-element.29) | copy-start | bytes 196612
  96.6 3.6 %copy-start.57 = (bf16[512,256]{1,0:T(8,128)(2,1)S(1)}, bf16[512,256]{1,0:T(8,128)(2,1)}, u32[]{:S(2)}) copy-start(bf16[512,256]{1,0:T(8,128)(2,1)} %convolution_convert_fusion.10) | copy-start | bytes 786436
  97.8 0.7 copy-start.18
  99.9 1.1 copy-start.16
  99.9 1.1 copy-start.50
  100.3 0.7 copy-start.52
  112.2 0.8 copy-start.1
  112.2 1.5 copy-start.13
  115.2 1.4 copy-start.22
  116.6 1.3 copy-start.9
  116.6 1.3 copy-start.11
  118.0 2.2 copy-start.28
  118.0 2.4 copy-start.17
  118.0 2.4 copy-start.43
  118.0 2.4 copy-start.45
  118.0 2.4 copy-start.47
  118.0 2.4 copy-start.51
  118.0 2.4 copy-start.53
  118.0 2.4 copy-start.58
  118.9 0.7 copy-start.4
  119.6 2.4 %copy-start.14 = (bf16[128,640,1]{1,0,2:T(8,128)(2,1)}, bf16[128,640,1]{1,0,2:T(8,128)(2,1)S(1)}, u32[]{:S(2)}) copy-start(bf16[128,640,1]{1,0,2:T(8,128)(2,1)S(1)} %fusion.57) | copy-start | bytes 491524
  120.1 1.9 copy-start.6
  120.4 1.6 copy-start.30
  120.4 1.6 copy-start.31
  122.0 0.9 copy-start.29
  122.0 0.9 copy-start.33
  122.0 0.9 copy-start.37
  122.0 1.6 copy-start.41
  123.0 1.6 copy-start.7
  123.7 2.3 copy-start.19
  124.1 1.9 copy-start.20
  124.1 12.2 %copy-start.27 = (f32[128,128]{1,0:T(8,128)S(1)}, f32[128,128]{1,0:T(8,128)}, u32[]{:S(2)}) copy-start(f32[128,128]{1,0:T(8,128)} %copy-done.26) | copy-start | bytes 196612
  124.6 12.5 %copy-start.3 = (f32[512,256]{1,0:T(8,128)S(1)}, f32[512,256]{1,0:T(8,128)}, u32[]{:S(2)}) copy-start(f32[512,256]{1,0:T(8,128)} %copy.27) | copy-start | bytes 1572868
  124.6 12.5 %copy-start.35 = (f32[256]{0:T(256)S(1)}, f32[256]{0:T(256)}, u32[]{:S(2)}) copy-start(f32[256]{0:T(256)} %copy-done.34) | copy-start | bytes 3076
  126.0 12.6 %copy-start.39 = (f32[128]{0:T(128)S(1)}, f32[128]{0:T(128)}, u32[]{:S(2)}) copy-start(f32[128]{0:T(128)} %copy-done.38) | copy-start | bytes 1540
  127.3 12.6 %copy-start.5 = (f32[128,640]{1,0:T(8,128)S(1)}, f32[128,640]{1,0:T(8,128)}, u32[]{:S(2)}) copy-start(f32[128,640]{1,0:T(8,128)} %copy-done.4) | copy-start | bytes 983044
  127.4 12.6 %copy-start.55 = (f32[128]{0:T(128)S(1)}, f32[128]{0:T(128)}, u32[]{:S(2)}) copy-start(f32[128]{0:T(128)} %get-tuple-element.69) | copy-start | bytes 1540
  127.4 13.4 %copy-start.21 = (bf16[128,4,256]{0,2,1:T(8,128)(2,1)S(1)}, bf16[128,4,256]{0,2,1:T(8,128)(2,1)}, u32[]{:S(2)}) copy-start(bf16[128,4,256]{0,2,1:T(8,128)(2,1)} %copy-done.20) | copy-start | bytes 786436
  138.6 6.3 %copy-start.8 = (bf16[4,128,256]{1,2,0:T(8,128)(2,1)S(1)}, bf16[4,128,256]{1,2,0:T(8,128)(2,1)}, u32[]{:S(2)}) copy-start(bf16[4,128,256]{1,2,0:T(8,128)(2,1)} %copy.28) | copy-start | bytes 786436
  138.6 6.3 %copy-start.15 = (bf16[128,640,1]{1,0,2:T(8,128)(2,1)S(1)}, bf16[128,640,1]{1,0,2:T(8,128)(2,1)}, u32[]{:S(2)}) copy-start(bf16[128,640,1]{1,0,2:T(8,128)(2,1)} %copy-done.14) | copy-start | bytes 491524
  140.8 5.6 %copy-start.12 = (bf16[128,2048]{1,0:T(8,128)(2,1)S(1)}, bf16[128,2048]{1,0:T(8,128)(2,1)}, u32[]{:S(2)}) copy-start(bf16[128,2048]{1,0:T(8,128)(2,1)} %copy-done.11) | copy-start | bytes 1572868
  147.4 1.8 copy-start.10
  150.1 2.1 copy-start.2
  150.1 2.0 copy-start.23
  153.0 2.0 copy-start.49
  153.0 2.4 %copy-start.48 = (bf16[640]{0:T(1024)(128)(2,1)S(1)}, bf16[640]{0:T(1024)(128)(2,1)}, u32[]{:S(2)}) copy-start(bf16[640]{0:T(1024)(128)(2,1)} %get-tuple-element.22) | copy-start | bytes 3844
  153.0 2.6 %copy-start.54 = (bf16[256]{0:T(256)(128)(2,1)S(1)}, bf16[256]{0:T(256)(128)(2,1)}, u32[]{:S(2)}) copy-start(bf16[256]{0:T(256)(128)(2,1)} %get-tuple-element.14) | copy-start | bytes 1540

commit v2 on v1

--- a/solution.py
+++ b/solution.py
@@ -206,6 +206,10 @@
         one.wait_send()
 
 
+def takes(microseconds):
+    return pl.CostEstimate(flops=0, transcendentals=0, bytes_accessed=microseconds * 3690000)
+
+
 def gather_call(packed, extra, devices, cycle):
     cut = packed.shape[0] // 32 * 16
     return pl.pallas_call(
@@ -224,11 +228,12 @@
             pltpu.SemaphoreType.DMA((2,)),
         ],
         compiler_params=pltpu.CompilerParams(collective_id=0, has_side_effects=True),
+        cost_estimate=takes(25),
         name="gather_weights",
     )(packed, extra)
 
 
-def reduce_kernel(cut, g_ref, out, cbuf, abuf, bbuf, zbuf, send, recv):
+def reduce_kernel(cut, g_ref, f_ref, out, fout, cbuf, abuf, bbuf, zbuf, fbuf, send, recv):
     z, x, y, c = coordinates()
     rows = g_ref.shape[1]
     part = (pl.ds(0, cut), pl.ds(cut, rows - cut))
@@ -269,6 +274,8 @@
     for k, a, b in far:
         i = place(k, a, b)
         push(i, g_ref.at[block(k, a, b, 1 - c)], cbuf.at[i], to_c)
+    for k in (2, 1, 3):
+        push(45 + k, f_ref.at[k], fbuf.at[k - 1], to_z[Z - k])
     for k, a, b in far:
         i = place(k, a, b)
         arrived(i, cbuf.at[i])
@@ -304,6 +311,10 @@
                     zbuf.at[k - 1, part[p]],
                     to_z[k],
                 )
+    fout[...] = f_ref[0].astype(F32)
+    for k in (1, 3, 2):
+        arrived(45 + k, fbuf.at[k - 1])
+        fout[...] = fout[...] + fbuf[k - 1].astype(F32)
     out[...] = bbuf[0].astype(F32)
     for k in (1, 3, 2):
         for p in range(2):
@@ -313,27 +324,32 @@
         one.wait_send()
 
 
-def reduce_call(terms):
+def reduce_call(terms, feed):
     shape = terms.shape[1:]
     cut = shape[0] // 32 * 16
     return pl.pallas_call(
         functools.partial(reduce_kernel, cut),
-        out_shape=jax.ShapeDtypeStruct(shape, F32),
-        in_specs=[pl.BlockSpec(memory_space=pltpu.VMEM)],
-        out_specs=pl.BlockSpec(memory_space=pltpu.VMEM),
+        out_shape=(
+            jax.ShapeDtypeStruct(shape, F32),
+            jax.ShapeDtypeStruct(feed.shape[1:], F32),
+        ),
+        in_specs=[pl.BlockSpec(memory_space=pltpu.VMEM)] * 2,
+        out_specs=[pl.BlockSpec(memory_space=pltpu.VMEM)] * 2,
         scratch_shapes=[
             pltpu.VMEM((16,) + shape, BF),
             pltpu.VMEM((8,) + shape, BF),
             pltpu.VMEM((4,) + shape, BF),
             pltpu.VMEM((3,) + shape, BF),
-            pltpu.SemaphoreType.DMA((46,)),
-            pltpu.SemaphoreType.DMA((46,)),
+            pltpu.VMEM((3,) + feed.shape[1:], BF),
+            pltpu.SemaphoreType.DMA((49,)),
+            pltpu.SemaphoreType.DMA((49,)),
         ],
         compiler_params=pltpu.CompilerParams(
-            collective_id=1, has_side_effects=True, vmem_limit_bytes=48 * 1024 * 1024
+            collective_id=1, has_side_effects=True, vmem_limit_bytes=32 * 1024 * 1024
         ),
+        cost_estimate=takes(28),
         name="reduce_gradients",
-    )(terms)
+    )(terms, feed)
 
 
 def exchange_kernel(g_ref, out, buf, send, recv):
@@ -376,8 +392,56 @@
         compiler_params=pltpu.CompilerParams(
             collective_id=2, has_side_effects=True, vmem_limit_bytes=16 * 1024 * 1024
         ),
+        cost_estimate=takes(9),
         name="exchange_keys",
     )(terms)
+
+
+def move(value, axis, to):
+    size = lax.axis_size(axis)
+    return lax.ppermute(value, axis, [(i, to(i)) for i in range(size)])
+
+
+def over_z(value, k):
+    return move(value, "dp", lambda i: (i // 2 + k) % Z * 2 + i % 2)
+
+
+def over_x(value):
+    return move(value, "dp", lambda i: i ^ 1)
+
+
+def over_y(value):
+    return move(value, "ctx", lambda i: i ^ 2)
+
+
+def over_core(value):
+    return move(value, "ctx", lambda i: i ^ 1)
+
+
+def halves(*pieces):
+    return jnp.concatenate([p.reshape(2, p.shape[0] // 2, D) for p in pieces], axis=1)
+
+
+def gather_feed(own):
+    line = jnp.stack([own] + [over_z(own, k) for k in (1, 2, 3)])
+    low, high = line[:, 0], line[:, 1]
+    low = jnp.stack([low, over_x(low)])
+    high = jnp.stack([high, over_y(high)])
+    low = jnp.stack([low, over_y(low)])
+    high = jnp.stack([high, over_x(high)])
+    return jnp.stack([jnp.stack([low, high]), jnp.stack([over_core(low), over_core(high)])])
+
+
+def reduce_over_core(terms):
+    return [terms[0, p] + over_core(terms[1, p]) for p in range(2)]
+
+
+def reduce_first(low, high):
+    return [low[0] + over_y(low[1]), high[0] + over_x(high[1])]
+
+
+def reduce_second(low, high):
+    return [low[0] + over_x(low[1]), high[0] + over_y(high[1])]
 
 
 def body(
@@ -391,7 +455,12 @@
     place = lax.axis_index("ctx")
     scale = HD ** (-0.5)
     doc_local = segments[0]
-    own = (w_query.T, w_key.T, w_value.T, w_out, w_gate.T, w_up.T, w_down)
+    own = (w_query.T, w_key.T, w_value.T, w_out)
+    if kernels:
+        feed = gather_feed(halves(w_gate.T, w_up.T, w_down))
+    else:
+        own += (w_gate.T, w_up.T, w_down)
+    weights_held = len(own)
     own += (jnp.pad(gains[None], ((0, 0), (0, D - gains.shape[0]))),)
     counts = [piece.shape[0] for piece in own]
     starts = [sum(counts[:i]) for i in range(len(counts))]
@@ -408,10 +477,15 @@
         every = lax.all_gather(packed, ("dp", "ctx"), axis=0, tiled=False)
         tokens_all = lax.all_gather(tokens[0], "ctx", axis=0, tiled=True)
         doc_all = lax.all_gather(doc_local, "ctx", axis=0, tiled=True)
-    wq, wk, wv, wo, wg, wu, wd = [
-        every[:, s : s + n].reshape(devices * n, D) for s, n in zip(starts[:7], counts[:7])
+    held = [
+        every[:, s : s + n].reshape(devices * n, D)
+        for s, n in zip(starts[:weights_held], counts[:weights_held])
     ]
-    gain_all = every[:, starts[7], : gains.shape[0]].reshape(-1).astype(F32)
+    if kernels:
+        third = feed.shape[-2] // 3
+        held += [feed[..., i * third : (i + 1) * third, :].reshape(-1, D) for i in range(3)]
+    wq, wk, wv, wo, wg, wu, wd = held
+    gain_all = every[:, starts[weights_held], : gains.shape[0]].reshape(-1).astype(F32)
     g_in = gain_all[0:D]
     g_post_attn = gain_all[D : 2 * D]
     g_pre_ff = gain_all[2 * D : 3 * D]
@@ -472,6 +546,12 @@
     grad_up = grad_up_f.astype(BF)
     w_gate_part = inner_rows(grad_gate, ff_in)
     w_up_part = inner_rows(grad_up, ff_in)
+    if kernels:
+        feed_terms = [w_gate_part, w_up_part, w_down_part]
+        shape = feed.shape[:-2] + (third, D)
+        feed_sum = jnp.concatenate([term.astype(BF).reshape(shape) for term in feed_terms], axis=-2)
+        feed_sum, grad_gate, grad_up = lax.optimization_barrier((feed_sum, grad_gate, grad_up))
+        feed_sum = reduce_over_core(feed_sum)
     grad_ff = product(grad_gate, wg) + product(grad_up, wu)
     hidden_part, grad_g_pre_ff = norm_backward(hidden, ff_factor, g_pre_ff, grad_ff)
     grad_hidden = grad_out + hidden_part
@@ -479,6 +559,9 @@
     grad_branch = grad_branch_f.astype(BF)
     w_out_part = inner_rows(heads, grad_branch)
     grad_att = against(grad_branch, wo).reshape(rows, H, HD).astype(BF)
+    if kernels:
+        feed_sum, grad_att = lax.optimization_barrier((feed_sum, grad_att))
+        feed_sum = reduce_first(*feed_sum)
     grad_rows = jnp.transpose(grad_att, (1, 0, 2)).reshape(H * rows, HD)
     delta = jnp.sum(grad_rows.astype(F32) * attended_rows, axis=1, keepdims=True)
     grad_probs = against(grad_rows, values_all)
@@ -489,6 +572,8 @@
     grad_kv = jnp.concatenate([grad_key_part, grad_value_part], axis=1)
     if kernels:
         key_grad = exchange_call(grad_kv.astype(BF).reshape(cycle, rows, 2 * HD))
+        feed_sum, key_grad = lax.optimization_barrier((feed_sum, key_grad))
+        feed_sum = reduce_second(*feed_sum)
     else:
         key_grad = lax.psum_scatter(grad_kv, "ctx", scatter_dimension=0, tiled=True)
     grad_krot = key_grad[:, :HD]
@@ -519,17 +604,23 @@
             w_gate_part,
             w_up_part,
             w_down_part,
-        )
+        )[:weights_held]
     ]
     tail = ((0, 0), (0, height - sum(counts)), (0, D - gains.shape[0]))
     terms.append(jnp.pad(gains_part, tail))
     kind = BF if kernels else F32
     stacked = jnp.concatenate([term.astype(kind) for term in terms], axis=1)
     if kernels:
-        owned = reduce_call(stacked)
+        low, high = feed_sum
+        owned, feed_owned = reduce_call(stacked, jnp.concatenate([low, high], axis=1))
+        feed_owned = feed_owned.reshape(2, -1, D)
     else:
         owned = lax.psum_scatter(stacked, ("dp", "ctx"), scatter_dimension=0, tiled=False)
-    q, k, v, o, g, u, d, s = [owned[a : a + n] for a, n in zip(starts, counts)]
+    parts = [owned[a : a + n] for a, n in zip(starts, counts)]
+    s = parts.pop()
+    if kernels:
+        parts += [feed_owned[:, i * third : (i + 1) * third].reshape(-1, D) for i in range(3)]
+    q, k, v, o, g, u, d = parts
     return (
         mixed[None],
         tokens_grad[None],

time: 239 us -> 251 us (1.050)
  Pallas kernels: 152 us -> 100 us
  waiting for transfers between devices: 0 us -> 37.7 us
  other arithmetic: 20.8 us -> 40.9 us
  starting transfers between devices: 0 us -> 10.9 us
  matrix products: 31.8 us -> 28.8 us
    pallas_call x1, Pallas kernels: 77.9 us -> 38.8 us  [reduce_call(): pl.pallas_call(functools.partial(reduce_kernel, cut), out_shape=(jax.Shap...]
    ppermute x0 -> x15, waiting for transfers between devices: none -> 37.7 us  [move(): return lax.ppermute(value, axis, [(i, to(i)) for i in range(size)])]
    pallas_call x1, Pallas kernels: 65.4 us -> 36.2 us  [gather_call(): pl.pallas_call(functools.partial(gather_kernel, cut), out_shape=(jax.Shap...]
    another operation x1 -> x10, other arithmetic: 1.9 us -> 19.1 us  [the longest x3 5.53 us: gather_feed(): jnp.stack([jnp.stack([low, high]), jnp.stack([over_core(low), over_core(h...]
    pallas_call x1, Pallas kernels: 8.88 us -> 25.3 us  [exchange_call(): pl.pallas_call(exchange_kernel, out_shape=jax.ShapeDtypeStruct(shape, F32...]
    ppermute x0 -> x15, starting transfers between devices: none -> 10.9 us  [move(): return lax.ppermute(value, axis, [(i, to(i)) for i in range(size)])]
    slice x2 -> x1, local copies, waits for them, and re-layouts: 5.96 us -> 1.99 us  [body(): every[:, s:s + n].reshape(devices * n, D)]
    add x0 -> x5, other arithmetic: none -> 3.47 us  [the longest x2 2.92 us: reduce_first(): return [low[0] + over_y(low[1]), high[0] + over_x(high[1])]]
  transfers between devices with their start and end apart: 0 -> 15, of which waited for: 0 -> 5; matrix products, arithmetic and copies ran while one was open for 0% -> 24% of each run, Pallas kernels for 0% -> 25%
where the time goes in v2:
time: 251 us; the launch traced here: 250 us
  Pallas kernels  100 us (40%)
  other arithmetic  40.9 us (16%)
  waiting for transfers between devices  37.7 us (15%)
  local copies, waits for them, and re-layouts  29.7 us (12%)
  matrix products  28.8 us (11%)
  starting transfers between devices  10.9 us (4%)
    pallas_call x1, Pallas kernels, reduce_call(): pl.pallas_call(functools.partial(reduce_kernel, cut), out_shape=(jax.Shap...  38.8 us
    ppermute x15, waiting for transfers between devices, move(): return lax.ppermute(value, axis, [(i, to(i)) for i in range(size)])  37.7 us
    pallas_call x1, Pallas kernels, gather_call(): pl.pallas_call(functools.partial(gather_kernel, cut), out_shape=(jax.Shap...  36.2 us
    pallas_call x1, Pallas kernels, exchange_call(): pl.pallas_call(exchange_kernel, out_shape=jax.ShapeDtypeStruct(shape, F32...  25.3 us
    unnamed x115, local copies, waits for them, and re-layouts  11.9 us
    ppermute x15, starting transfers between devices, move(): return lax.ppermute(value, axis, [(i, to(i)) for i in range(size)])  10.9 us
    dot_general x10, matrix products, product(): return jnp.dot(left, right, preferred_element_type=F32)  10.1 us
    dot_general x9, matrix products, inner_rows(): lax.dot_general(left, right, (((0,), (0,)), ((), ())), preferred_element_...  9.65 us
  transfers between devices with their start and end apart: 15, of which 5 were waited for; matrix products, arithmetic and copies ran while one was open for 24% of the time, Pallas kernels for 25%

profile of v2, /device:TPU:0, one launch (start us, length us, event | category | flops | bytes accessed | tf_op | source)
XLA Modules:
  0.0 250.1 jit_solution(15314830569300316268)
XLA Ops:
  0.6 1.8 fusion.67
  2.4 5.0 %collective-permute-start.2 = (bf16[2,96,640]{2,1,0:T(8,128)(2,1)}, bf16[2,96,640]{2,1,0:T(8,128)(2,1)}, u32[]{:S(2)}, u32[]{:S(2)}) collective-permute-start(bf16[2,96,640]{2,1,0:T(8,128)(2,1)} %get-tuple-element.98), channel_id=1, source_target_pairs={{0,24},{4,28},{8,0},{12,4},{16,8},{20,12},{24,16},{28,20},{1,25},{... | collective-permute-start | bytes 737288 | tf_op jit(solution)/shard_map/ppermute | solution.py:402
  7.5 1.0 collective-permute-start
  13.5 1.6 fusion.54.t_ref
  15.1 36.2 %gather_weights.1 = (bf16[32,96,640]{2,1,0:T(8,128)(2,1)}, bf16[4,144,640]{2,1,0:T(8,128)(2,1)}) custom-call(bf16[96,640]{1,0:T(8,128)(2,1)} %pad.18.w_ref, bf16[144,640]{1,0:T(8,128)(2,1)} %fusion.54.t_ref), custom_call_target="tpu_custom_call" | custom-call | bytes 92250000 | tf_op jit(solution)/shard_map/gather_weights/pallas_call | solution.py:215
  51.3 0.9 convert_reduce_fusion
  52.2 2.0 fusion.79
  54.5 1.3 fusion.4
  56.3 1.3 fusion.6
  58.9 2.2 multiply_reduce_fusion.3
  61.1 2.0 copy.28
  63.2 1.2 multiply_multiply_fusion.3
  64.3 1.8 subtract_convert_fusion.4
  67.0 1.5 pad_maximum_fusion.4
  68.5 1.2 slice_bitcast_fusion.8
  70.1 0.9 multiply_subtract_fusion.1
  71.9 11.4 %collective-permute-done.5 = bf16[4,96,640]{2,1,0:T(8,128)(2,1)S(1)} collective-permute-done((bf16[4,96,640]{2,1,0:T(8,128)(2,1)S(1)}, bf16[4,96,640]{2,1,0:T(8,128)(2,1)S(1)}, u32[]{:S(2)}, u32[]{:S(2)}) %collective-permute-start.5) | collective-permute-done | bytes 491552 | tf_op jit(solution)/shard_map/ppermute | solution.py:402
  83.2 1.4 fusion.74
  84.8 1.4 fusion.75
  86.2 1.4 collective-permute-start.4
  89.2 1.4 convolution_convert_fusion.10
  90.5 17.9 %collective-permute-done.6 = bf16[2,4,96,640]{3,2,1,0:T(8,128)(2,1)} collective-permute-done((bf16[2,4,96,640]{3,2,1,0:T(8,128)(2,1)}, bf16[2,4,96,640]{3,2,1,0:T(8,128)(2,1)}, u32[]{:S(2)}, u32[]{:S(2)}) %collective-permute-start.6) | collective-permute-done | bytes 983072 | tf_op jit(solution)/shard_map/ppermute | solution.py:402
  108.4 3.5 %pad_maximum_fusion.3 = (bf16[2,2,4,96,640]{4,3,2,1,0:T(8,128)(2,1)}, bf16[1,2,2,4,96,640]{5,4,3,2,1,0:T(8,128)(2,1)}) fusion(bf16[1,2,4,96,640]{4,3,2,1,0:T(8,128)(2,1)} %bitcast.40, bf16[1,2,4,96,640]{4,3,2,1,0:T(8,128)(2,1)S(1)} %copy-done.7), kind=kLoop, calls=%fused_computation.14 | loop fusion | flops 983040 | bytes 5898240 | tf_op jit(solution)/shard_map/stack | solution.py:431
  112.0 2.2 pad_maximum_fusion.2
  115.4 1.6 fusion.84
  117.0 1.8 copy.29
  118.8 1.6 multiply_reduce_fusion.11
  120.8 2.0 maximum_bitcast_fusion
  122.8 2.5 %maximum_bitcast_fusion.1 = bf16[1,2,2,2,4,96,640]{6,5,4,3,2,1,0:T(8,128)(2,1)S(1)} fusion(bf16[1,2,2,4,96,640]{5,4,3,2,1,0:T(8,128)(2,1)} %bitcast.44, bf16[1,2,2,4,96,640]{5,4,3,2,1,0:T(8,128)(2,1)} %bitcast.43), kind=kLoop, calls=%fused_computation.6 | loop fusion | flops 1966080 | bytes 7864320 | tf_op jit(solution)/shard_map/stack | solution.py:432
  125.3 1.0 pad_maximum_fusion.1
  126.4 1.0 fusion.85
  127.3 1.0 multiply_convert_fusion.2
  129.9 0.8 fusion.30
  130.8 0.9 convolution_convert_fusion
  131.7 1.4 fusion.15
  133.0 0.9 convolution_convert_fusion.1
  133.9 0.9 convolution_convert_fusion.2
  134.8 0.9 pad_maximum_fusion
  138.0 1.2 multiply_reduce_fusion.5
  139.2 0.8 multiply_reduce_fusion.6
  140.9 2.2 collective-permute-done.9
  145.0 0.8 convolution_multiply_fusion
  145.9 1.1 slice_bitcast_fusion.3
  147.4 1.0 slice_bitcast_fusion.2
  150.4 0.9 copy.31
  151.3 25.3 %exchange_keys.1 = f32[128,512]{1,0:T(8,128)S(1)} custom-call(bf16[4,128,512]{2,1,0:T(8,128)(2,1)S(1)} %pad_maximum_fusion.9.g_ref), custom_call_target="tpu_custom_call" | custom-call | bytes 33210000 | tf_op jit(solution)/shard_map/exchange_keys/pallas_call | solution.py:382
  176.7 2.7 %fusion.3 = bf16[32,96,640]{2,1,0:T(8,128)(2,1)} fusion(bf16[32,32,128]{2,1,0:T(8,128)(2,1)} %bitcast.269, bf16[1,128,640]{2,1,0:T(8,128)(2,1)S(1)} %copy-done.1, f32[640]{0:T(1024)S(1)} %get-tuple-element.102, f32[128]{0:T(128)} %copy-done.32), kind=kOutput, calls=%fused_computation.24 | convolution fusion | flops 168755200 | bytes 1739776 | tf_op jit(solution)/shard_map/dot_general | solution.py:57
  179.8 1.6 bitcast_add_fusion.3
  181.4 1.4 bitcast_add_fusion.2
  183.6 1.2 convolution_add_fusion.2
  184.9 1.3 fusion.41
  186.4 1.4 dynamic-update-slice.5
  187.9 1.4 dynamic-update-slice.6
  189.3 1.4 dynamic-update-slice.7
  190.7 1.4 dynamic-update-slice.8
  192.2 1.3 dynamic-update-slice.9
  193.5 1.3 dynamic-update-slice.10
  196.7 1.1 fusion.8
  197.8 1.1 fusion.7
  198.8 1.6 fusion.2
  200.4 0.9 pad_dynamic-update-slice_fusion.g_ref
  201.4 0.8 fusion.60
  202.2 6.0 %collective-permute-done.14 = bf16[4,96,640]{2,1,0:T(8,128)(2,1)S(1)} collective-permute-done((bf16[4,96,640]{2,1,0:T(8,128)(2,1)S(1)}, bf16[4,96,640]{2,1,0:T(8,128)(2,1)S(1)}, u32[]{:S(2)}, u32[]{:S(2)}) %collective-permute-start.14) | collective-permute-done | bytes 491552 | tf_op jit(solution)/shard_map/ppermute | solution.py:402
  208.7 38.8 %reduce_gradients.1 = (f32[96,640]{1,0:T(8,128)S(1)}, f32[192,640]{1,0:T(8,128)S(1)}) custom-call(bf16[32,96,640]{2,1,0:T(8,128)(2,1)S(1)} %copy-done, bf16[4,192,640]{2,1,0:T(8,128)(2,1)S(1)} %pad_maximum_fusion.7.f_ref), custom_call_target="tpu_custom_call" | custom-call | bytes 103320000 | tf_op jit(solution)/shard_map/reduce_gradients/pallas_call | solution.py:330
  (201 shorter events, 27.5 us)
Async XLA Ops:
  2.4 64.6 %collective-permute-start.2 = (bf16[2,96,640]{2,1,0:T(8,128)(2,1)}, bf16[2,96,640]{2,1,0:T(8,128)(2,1)}, u32[]{:S(2)}, u32[]{:S(2)}) collective-permute-start(bf16[2,96,640]{2,1,0:T(8,128)(2,1)} %get-tuple-element.98), channel_id=1, source_target_pairs={{0,24},{4,28},{8,0},{12,4},{16,8},{20,12},{24,16},{28,20},{1,25},{... | collective-permute-start | bytes 737288 | tf_op jit(solution)/shard_map/ppermute | solution.py:402
  7.5 59.5 %collective-permute-start.1 = (bf16[2,96,640]{2,1,0:T(8,128)(2,1)}, bf16[2,96,640]{2,1,0:T(8,128)(2,1)}, u32[]{:S(2)}, u32[]{:S(2)}) collective-permute-start(bf16[2,96,640]{2,1,0:T(8,128)(2,1)} %get-tuple-element.98), channel_id=1, source_target_pairs={{0,16},{4,20},{8,24},{12,28},{16,0},{20,4},{24,8},{28,12},{1,17},{... | collective-permute-start | bytes 737288 | tf_op jit(solution)/shard_map/ppermute | solution.py:402
  7.5 59.5 %collective-permute-start = (bf16[2,96,640]{2,1,0:T(8,128)(2,1)}, bf16[2,96,640]{2,1,0:T(8,128)(2,1)}, u32[]{:S(2)}, u32[]{:S(2)}) collective-permute-start(bf16[2,96,640]{2,1,0:T(8,128)(2,1)} %get-tuple-element.98), channel_id=1, source_target_pairs={{0,8},{4,12},{8,16},{12,20},{16,24},{20,28},{24,0},{28,4},{1,9},{5... | collective-permute-start | bytes 737288 | tf_op jit(solution)/shard_map/ppermute | solution.py:402
  52.2 2.0 copy-start.1
  54.5 12.4 %copy-start.30 = (f32[256]{0:T(256)}, f32[256]{0:T(256)S(1)}, u32[]{:S(2)}) copy-start(f32[256]{0:T(256)S(1)} %get-tuple-element.104) | copy-start | bytes 3076
  56.3 2.0 copy-start.32
  57.6 1.3 copy-start.20
  66.2 21.5 %copy-start.26 = (bf16[512,128]{1,0:T(8,128)(2,1)}, bf16[512,128]{1,0:T(8,128)(2,1)S(1)}, u32[]{:S(2)}) copy-start(bf16[512,128]{1,0:T(8,128)(2,1)S(1)} %get-tuple-element.84) | copy-start | bytes 393220
  66.8 3.3 %copy-start.22 = (f32[128,128]{1,0:T(8,128)}, f32[128,128]{1,0:T(8,128)S(1)}, u32[]{:S(2)}) copy-start(f32[128,128]{1,0:T(8,128)S(1)} %get-tuple-element.51) | copy-start | bytes 196612
  69.6 15.1 %copy-start.50 = (s32[1,128]{1,0:T(1,128)S(1)}, s32[1,128]{1,0:T(1,128)}, u32[]{:S(2)}) copy-start(s32[1,128]{1,0:T(1,128)} %param.13) | copy-start | bytes 1540
  69.6 13.6 %collective-permute-start.5 = (bf16[4,96,640]{2,1,0:T(8,128)(2,1)S(1)}, bf16[4,96,640]{2,1,0:T(8,128)(2,1)S(1)}, u32[]{:S(2)}, u32[]{:S(2)}) collective-permute-start(bf16[4,96,640]{2,1,0:T(8,128)(2,1)S(1)} %get-tuple-element.75), channel_id=1, source_target_pairs={{0,2},{1,3},{2,0},{3,1},{4,6},{5,7},{6,4},{7,5},{8,10},{9,11},{10,... | collective-permute-start | bytes 1474568 | tf_op jit(solution)/shard_map/ppermute | solution.py:402
  71.0 13.7 %collective-permute-start.3 = (bf16[4,96,640]{2,1,0:T(8,128)(2,1)}, bf16[4,96,640]{2,1,0:T(8,128)(2,1)}, u32[]{:S(2)}, u32[]{:S(2)}) collective-permute-start(bf16[4,96,640]{2,1,0:T(8,128)(2,1)} %get-tuple-element.77), channel_id=1, source_target_pairs={{0,4},{4,0},{8,12},{12,8},{16,20},{20,16},{24,28},{28,24},{1,5},{5... | collective-permute-start | bytes 1474568 | tf_op jit(solution)/shard_map/ppermute | solution.py:402
  71.9 43.4 %copy-start.36 = (s32[4,1,128]{2,1,0:T(1,128)}, s32[4,1,128]{2,1,0:T(1,128)S(1)}, u32[]{:S(2)}) copy-start(s32[4,1,128]{2,1,0:T(1,128)S(1)} %slice_convert_fusion.2) | copy-start | bytes 6148
  84.7 23.8 %collective-permute-start.6 = (bf16[2,4,96,640]{3,2,1,0:T(8,128)(2,1)}, bf16[2,4,96,640]{3,2,1,0:T(8,128)(2,1)}, u32[]{:S(2)}, u32[]{:S(2)}) collective-permute-start(bf16[2,4,96,640]{3,2,1,0:T(8,128)(2,1)} %get-tuple-element.79), channel_id=1, source_target_pairs={{0,4},{4,0},{8,12},{12,8},{16,20},{20,16},{24,28},{28,24},{1,5},{5... | collective-permute-start | bytes 2949128 | tf_op jit(solution)/shard_map/ppermute | solution.py:402
  84.7 30.6 %copy-start.38 = (s32[512]{0:T(512)}, s32[512]{0:T(512)S(1)}, u32[]{:S(2)}) copy-start(s32[512]{0:T(512)S(1)} %get-tuple-element.135) | copy-start | bytes 6148
  84.7 30.6 %copy-start.40 = (s32[512]{0:T(512)}, s32[512]{0:T(512)S(1)}, u32[]{:S(2)}) copy-start(s32[512]{0:T(512)S(1)} %get-tuple-element.136) | copy-start | bytes 6148
  84.7 2.9 %copy-start.17 = (f32[128,4,128]{2,0,1:T(8,128)S(1)}, f32[128,4,128]{2,0,1:T(8,128)}, u32[]{:S(2)}) copy-start(f32[128,4,128]{2,0,1:T(8,128)} %get-tuple-element.82) | copy-start | bytes 786436
  84.7 2.9 %copy-start.18 = (f32[128,4,128]{2,0,1:T(8,128)S(1)}, f32[128,4,128]{2,0,1:T(8,128)}, u32[]{:S(2)}) copy-start(f32[128,4,128]{2,0,1:T(8,128)} %get-tuple-element.83) | copy-start | bytes 786436
  84.7 3.6 %copy-start.28 = (bf16[512,128]{1,0:T(8,128)(2,1)S(1)}, bf16[512,128]{1,0:T(8,128)(2,1)}, u32[]{:S(2)}) copy-start(bf16[512,128]{1,0:T(8,128)(2,1)} %get-tuple-element.85) | copy-start | bytes 393220
  86.1 3.0 %copy-start.21 = (bf16[4,128,640]{2,1,0:T(8,128)(2,1)S(1)}, bf16[4,128,640]{2,1,0:T(8,128)(2,1)}, u32[]{:S(2)}) copy-start(bf16[4,128,640]{2,1,0:T(8,128)(2,1)} %copy-done.20) | copy-start | bytes 1966084
  86.2 25.8 %collective-permute-start.4 = (bf16[2,4,96,640]{3,2,1,0:T(8,128)(2,1)S(1)}, bf16[2,4,96,640]{3,2,1,0:T(8,128)(2,1)S(1)}, u32[]{:S(2)}, u32[]{:S(2)}) collective-permute-start(bf16[2,4,96,640]{3,2,1,0:T(8,128)(2,1)S(1)} %get-tuple-element.73), channel_id=1, source_target_pairs={{0,2},{1,3},{2,0},{3,1},{4,6},{5,7},{6,4},{7,5},{8,10},{9,11},{10,... | collective-permute-start | bytes 2949128 | tf_op jit(solution)/shard_map/ppermute | solution.py:402
  87.6 20.9 %copy-start.7 = (bf16[1,2,4,96,640]{4,3,2,1,0:T(8,128)(2,1)S(1)}, bf16[1,2,4,96,640]{4,3,2,1,0:T(8,128)(2,1)}, u32[]{:S(2)}) copy-start(bf16[1,2,4,96,640]{4,3,2,1,0:T(8,128)(2,1)} %get-tuple-element.78) | copy-start | bytes 2949124
  88.7 26.6 %copy-start.13 = (f32[512,512]{0,1:T(8,128)}, f32[512,512]{0,1:T(8,128)S(1)}, u32[]{:S(2)}) copy-start(f32[512,512]{0,1:T(8,128)S(1)} %get-tuple-element.122) | copy-start | bytes 3145732
  88.7 26.6 %copy-start.43 = (f32[512]{0:T(512)}, f32[512]{0:T(512)S(1)}, u32[]{:S(2)}) copy-start(f32[512]{0:T(512)S(1)} %get-tuple-element.121) | copy-start | bytes 6148
  89.1 26.2 %copy-start.45 = (f32[512]{0:T(512)}, f32[512]{0:T(512)S(1)}, u32[]{:S(2)}) copy-start(f32[512]{0:T(512)S(1)} %fusion.55) | copy-start | bytes 6148
  90.5 24.9 %copy-start.51 = (bf16[512,256]{1,0:T(8,128)(2,1)}, bf16[512,256]{1,0:T(8,128)(2,1)S(1)}, u32[]{:S(2)}) copy-start(bf16[512,256]{1,0:T(8,128)(2,1)S(1)} %convolution_convert_fusion.10) | copy-start | bytes 786436
  111.9 10.8 %collective-permute-start.8 = (bf16[2,2,4,96,640]{4,3,2,1,0:T(8,128)(2,1)}, bf16[2,2,4,96,640]{4,3,2,1,0:T(8,128)(2,1)}, u32[]{:S(2)}, u32[]{:S(2)}) collective-permute-start(bf16[2,2,4,96,640]{4,3,2,1,0:T(8,128)(2,1)} %get-tuple-element.68), channel_id=1, source_target_pairs={{0,1},{1,0},{2,3},{3,2},{4,5},{5,4},{6,7},{7,6},{8,9},{9,8},{10,11... | collective-permute-start | bytes 5898248 | tf_op jit(solution)/shard_map/ppermute | solution.py:402
  114.1 8.6 %collective-permute-start.7 = (bf16[2,2,4,96,640]{4,3,2,1,0:T(8,128)(2,1)}, bf16[2,2,4,96,640]{4,3,2,1,0:T(8,128)(2,1)}, u32[]{:S(2)}, u32[]{:S(2)}) collective-permute-start(bf16[2,2,4,96,640]{4,3,2,1,0:T(8,128)(2,1)} %get-tuple-element.66), channel_id=1, source_target_pairs={{0,1},{1,0},{2,3},{3,2},{4,5},{5,4},{6,7},{7,6},{8,9},{9,8},{10,11... | collective-permute-start | bytes 5898248 | tf_op jit(solution)/shard_map/ppermute | solution.py:402
  118.8 1.9 copy-start.6
  136.2 4.7 %collective-permute-start.10 = (bf16[2,2,4,96,640]{4,3,2,1,0:T(8,128)(2,1)S(1)}, bf16[2,2,4,96,640]{4,3,2,1,0:T(8,128)(2,1)S(1)}, u32[]{:S(2)}, u32[]{:S(2)}) collective-permute-start(bf16[2,2,4,96,640]{4,3,2,1,0:T(8,128)(2,1)S(1)} %get-tuple-element.57), channel_id=1, source_target_pairs={{0,1},{1,0},{2,3},{3,2},{4,5},{5,4},{6,7},{7,6},{8,9},{9,8},{10,11... | collective-permute-start | bytes 5898248 | tf_op jit(solution)/shard_map/ppermute | solution.py:402
  136.3 6.8 %collective-permute-start.9 = (bf16[2,2,4,96,640]{4,3,2,1,0:T(8,128)(2,1)S(1)}, bf16[2,2,4,96,640]{4,3,2,1,0:T(8,128)(2,1)S(1)}, u32[]{:S(2)}, u32[]{:S(2)}) collective-permute-start(bf16[2,2,4,96,640]{4,3,2,1,0:T(8,128)(2,1)S(1)} %get-tuple-element.58), channel_id=1, source_target_pairs={{0,1},{1,0},{2,3},{3,2},{4,5},{5,4},{6,7},{7,6},{8,9},{9,8},{10,11... | collective-permute-start | bytes 5898248 | tf_op jit(solution)/shard_map/ppermute | solution.py:402
  140.8 2.7 %copy-start.24 = (f32[512,256]{1,0:T(8,128)S(1)}, f32[512,256]{1,0:T(8,128)}, u32[]{:S(2)}) copy-start(f32[512,256]{1,0:T(8,128)} %get-tuple-element.124) | copy-start | bytes 1572868
  140.8 2.9 %copy-start.14 = (f32[512,512]{0,1:T(8,128)S(1)}, f32[512,512]{0,1:T(8,128)}, u32[]{:S(2)}) copy-start(f32[512,512]{0,1:T(8,128)} %copy-done.13) | copy-start | bytes 3145732
  140.8 2.9 %copy-start.37 = (s32[4,1,128]{2,1,0:T(1,128)S(1)}, s32[4,1,128]{2,1,0:T(1,128)}, u32[]{:S(2)}) copy-start(s32[4,1,128]{2,1,0:T(1,128)} %copy-done.36) | copy-start | bytes 6148
  140.8 2.9 %copy-start.39 = (s32[512]{0:T(512)S(1)}, s32[512]{0:T(512)}, u32[]{:S(2)}) copy-start(s32[512]{0:T(512)} %copy-done.38) | copy-start | bytes 6148
  140.8 2.9 %copy-start.41 = (s32[512]{0:T(512)S(1)}, s32[512]{0:T(512)}, u32[]{:S(2)}) copy-start(s32[512]{0:T(512)} %copy-done.40) | copy-start | bytes 6148
  140.8 2.9 %copy-start.44 = (f32[512]{0:T(512)S(1)}, f32[512]{0:T(512)}, u32[]{:S(2)}) copy-start(f32[512]{0:T(512)} %copy-done.43) | copy-start | bytes 6148
  140.8 2.9 %copy-start.46 = (f32[512]{0:T(512)S(1)}, f32[512]{0:T(512)}, u32[]{:S(2)}) copy-start(f32[512]{0:T(512)} %copy-done.45) | copy-start | bytes 6148
  140.8 2.9 %copy-start.52 = (bf16[512,256]{1,0:T(8,128)(2,1)S(1)}, bf16[512,256]{1,0:T(8,128)(2,1)}, u32[]{:S(2)}) copy-start(bf16[512,256]{1,0:T(8,128)(2,1)} %copy-done.51) | copy-start | bytes 786436
  143.5 2.4 copy-start.4
  143.5 4.0 %copy-start.2 = (bf16[2,2,4,96,640]{4,3,2,1,0:T(8,128)(2,1)}, bf16[2,2,4,96,640]{4,3,2,1,0:T(8,128)(2,1)S(1)}, u32[]{:S(2)}) copy-start(bf16[2,2,4,96,640]{4,3,2,1,0:T(8,128)(2,1)S(1)} %get-tuple-element.30) | copy-start | bytes 5898244
  143.7 1.3 copy-start.29
  145.8 2.9 %copy-start.25 = (f32[128,128]{1,0:T(8,128)S(1)}, f32[128,128]{1,0:T(8,128)}, u32[]{:S(2)}) copy-start(f32[128,128]{1,0:T(8,128)} %get-tuple-element.50) | copy-start | bytes 196612
  145.8 3.0 %copy-start.31 = (f32[256]{0:T(256)S(1)}, f32[256]{0:T(256)}, u32[]{:S(2)}) copy-start(f32[256]{0:T(256)} %copy-done.30) | copy-start | bytes 3076
  146.9 2.9 %copy-start.16 = (bf16[128,4,256]{2,0,1:T(8,128)(2,1)S(1)}, bf16[128,4,256]{2,0,1:T(8,128)(2,1)}, u32[]{:S(2)}) copy-start(bf16[128,4,256]{2,0,1:T(8,128)(2,1)} %copy-done.15) | copy-start | bytes 786436
  146.9 32.9 %collective-permute-start.11 = (bf16[2,4,96,640]{3,2,1,0:T(8,128)(2,1)}, bf16[2,4,96,640]{3,2,1,0:T(8,128)(2,1)}, u32[]{:S(2)}, u32[]{:S(2)}) collective-permute-start(bf16[2,4,96,640]{3,2,1,0:T(8,128)(2,1)} %slice_bitcast_fusion.3), channel_id=1, source_target_pairs={{0,2},{1,3},{2,0},{3,1},{4,6},{5,7},{6,4},{7,5},{8,10},{9,11},{10,... | collective-permute-start | bytes 2949128 | tf_op jit(solution)/shard_map/ppermute | solution.py:402
  148.5 1.7 copy-start.35
  148.5 32.9 %collective-permute-start.12 = (bf16[2,4,96,640]{3,2,1,0:T(8,128)(2,1)}, bf16[2,4,96,640]{3,2,1,0:T(8,128)(2,1)}, u32[]{:S(2)}, u32[]{:S(2)}) collective-permute-start(bf16[2,4,96,640]{3,2,1,0:T(8,128)(2,1)} %slice_bitcast_fusion.2), channel_id=1, source_target_pairs={{0,4},{4,0},{8,12},{12,8},{16,20},{20,16},{24,28},{28,24},{1,5},{5... | collective-permute-start | bytes 2949128 | tf_op jit(solution)/shard_map/ppermute | solution.py:402
  151.3 28.1 %copy-start.19 = (bf16[128,4,256]{0,2,1:T(8,128)(2,1)S(1)}, bf16[128,4,256]{0,2,1:T(8,128)(2,1)}, u32[]{:S(2)}) copy-start(bf16[128,4,256]{0,2,1:T(8,128)(2,1)} %copy.31) | copy-start | bytes 786436
  151.3 28.5 %copy-start.5 = (bf16[2,2,4,96,640]{4,3,2,1,0:T(8,128)(2,1)S(1)}, bf16[2,2,4,96,640]{4,3,2,1,0:T(8,128)(2,1)}, u32[]{:S(2)}) copy-start(bf16[2,2,4,96,640]{4,3,2,1,0:T(8,128)(2,1)} %copy-done.4) | copy-start | bytes 5898244
  179.3 2.1 copy-start.3
  179.8 3.0 %copy-start.23 = (f32[128,128]{1,0:T(8,128)S(1)}, f32[128,128]{1,0:T(8,128)}, u32[]{:S(2)}) copy-start(f32[128,128]{1,0:T(8,128)} %copy-done.22) | copy-start | bytes 196612
  179.8 3.1 %copy-start.8 = (f32[512,256]{1,0:T(8,128)S(1)}, f32[512,256]{1,0:T(8,128)}, u32[]{:S(2)}) copy-start(f32[512,256]{1,0:T(8,128)} %copy.28) | copy-start | bytes 1572868
  179.8 3.1 %copy-start.42 = (f32[128]{0:T(128)S(1)}, f32[128]{0:T(128)}, u32[]{:S(2)}) copy-start(f32[128]{0:T(128)} %get-tuple-element.49) | copy-start | bytes 1540
  179.8 3.7 %copy-start.48 = (f32[128]{0:T(128)S(1)}, f32[128]{0:T(128)}, u32[]{:S(2)}) copy-start(f32[128]{0:T(128)} %get-tuple-element.48) | copy-start | bytes 1540
  181.4 3.5 %copy-start.33 = (f32[128]{0:T(128)S(1)}, f32[128]{0:T(128)}, u32[]{:S(2)}) copy-start(f32[128]{0:T(128)} %copy-done.32) | copy-start | bytes 1540
  181.4 7.9 %copy-start.34 = (bf16[640]{0:T(1024)(128)(2,1)S(1)}, bf16[640]{0:T(1024)(128)(2,1)}, u32[]{:S(2)}) copy-start(bf16[640]{0:T(1024)(128)(2,1)} %get-tuple-element.40) | copy-start | bytes 3844
  183.6 9.9 %copy-start.47 = (bf16[256]{0:T(256)(128)(2,1)S(1)}, bf16[256]{0:T(256)(128)(2,1)}, u32[]{:S(2)}) copy-start(bf16[256]{0:T(256)(128)(2,1)} %get-tuple-element.38) | copy-start | bytes 1540
  183.6 15.2 %copy-start.11 = (bf16[4,128,256]{1,2,0:T(8,128)(2,1)S(1)}, bf16[4,128,256]{1,2,0:T(8,128)(2,1)}, u32[]{:S(2)}) copy-start(bf16[4,128,256]{1,2,0:T(8,128)(2,1)} %copy.29) | copy-start | bytes 786436
  195.6 5.7 %copy-start.10 = (f32[128,640]{1,0:T(8,128)S(1)}, f32[128,640]{1,0:T(8,128)}, u32[]{:S(2)}) copy-start(f32[128,640]{1,0:T(8,128)} %copy-done.9) | copy-start | bytes 983044
  195.6 5.7 %copy-start.49 = (f32[128]{0:T(128)S(1)}, f32[128]{0:T(128)}, u32[]{:S(2)}) copy-start(f32[128]{0:T(128)} %get-tuple-element.109) | copy-start | bytes 1540
  195.7 12.5 %collective-permute-start.14 = (bf16[4,96,640]{2,1,0:T(8,128)(2,1)S(1)}, bf16[4,96,640]{2,1,0:T(8,128)(2,1)S(1)}, u32[]{:S(2)}, u32[]{:S(2)}) collective-permute-start(bf16[4,96,640]{2,1,0:T(8,128)(2,1)S(1)} %slice_bitcast_fusion.4), channel_id=1, source_target_pairs={{0,2},{1,3},{2,0},{3,1},{4,6},{5,7},{6,4},{7,5},{8,10},{9,11},{10,... | collective-permute-start | bytes 1474568 | tf_op jit(solution)/shard_map/ppermute | solution.py:402
  196.3 12.2 %collective-permute-start.13 = (bf16[4,96,640]{2,1,0:T(8,128)(2,1)S(1)}, bf16[4,96,640]{2,1,0:T(8,128)(2,1)S(1)}, u32[]{:S(2)}, u32[]{:S(2)}) collective-permute-start(bf16[4,96,640]{2,1,0:T(8,128)(2,1)S(1)} %slice_bitcast_fusion.5), channel_id=1, source_target_pairs={{0,4},{4,0},{8,12},{12,8},{16,20},{20,16},{24,28},{28,24},{1,5},{5... | collective-permute-start | bytes 1474568 | tf_op jit(solution)/shard_map/ppermute | solution.py:402
  202.2 6.5 %copy-start = (bf16[32,96,640]{2,1,0:T(8,128)(2,1)S(1)}, bf16[32,96,640]{2,1,0:T(8,128)(2,1)}, u32[]{:S(2)}) copy-start(bf16[32,96,640]{2,1,0:T(8,128)(2,1)} %pad_dynamic-update-slice_fusion.g_ref) | copy-start | bytes 11796484
  (4 other events, 3.5 us)

commit v3 on v1

--- a/solution.py
+++ b/solution.py
@@ -228,7 +228,7 @@
     )(packed, extra)
 
 
-def reduce_kernel(cut, g_ref, out, cbuf, abuf, bbuf, zbuf, send, recv):
+def reduce_kernel(cut, g_ref, out, lbuf, cbuf, abuf, bbuf, zbuf, send, recv, local):
     z, x, y, c = coordinates()
     rows = g_ref.shape[1]
     part = (pl.ds(0, cut), pl.ds(cut, rows - cut))
@@ -269,10 +269,16 @@
     for k, a, b in far:
         i = place(k, a, b)
         push(i, g_ref.at[block(k, a, b, 1 - c)], cbuf.at[i], to_c)
+    held = {}
+    for k, a, b in far:
+        i = place(k, a, b)
+        held[i] = pltpu.make_async_copy(g_ref.at[block(k, a, b, c)], lbuf.at[i], local.at[i])
+        held[i].start()
     for k, a, b in far:
         i = place(k, a, b)
         arrived(i, cbuf.at[i])
-        cbuf[i] = cbuf[i] + g_ref[block(k, a, b, c)]
+        held[i].wait()
+        cbuf[i] = cbuf[i] + lbuf[i]
         if b:
             j = k * 2 + a
             push(16 + j * 2, cbuf.at[i, part[0]], abuf.at[j, part[0]], to_y)
@@ -319,18 +325,20 @@
     return pl.pallas_call(
         functools.partial(reduce_kernel, cut),
         out_shape=jax.ShapeDtypeStruct(shape, F32),
-        in_specs=[pl.BlockSpec(memory_space=pltpu.VMEM)],
+        in_specs=[pl.BlockSpec(memory_space=pl.ANY)],
         out_specs=pl.BlockSpec(memory_space=pltpu.VMEM),
         scratch_shapes=[
+            pltpu.VMEM((16,) + shape, BF),
             pltpu.VMEM((16,) + shape, BF),
             pltpu.VMEM((8,) + shape, BF),
             pltpu.VMEM((4,) + shape, BF),
             pltpu.VMEM((3,) + shape, BF),
             pltpu.SemaphoreType.DMA((46,)),
             pltpu.SemaphoreType.DMA((46,)),
+            pltpu.SemaphoreType.DMA((16,)),
         ],
         compiler_params=pltpu.CompilerParams(
-            collective_id=1, has_side_effects=True, vmem_limit_bytes=48 * 1024 * 1024
+            collective_id=1, has_side_effects=True, vmem_limit_bytes=26 * 1024 * 1024
         ),
         name="reduce_gradients",
     )(terms)

time: 239 us -> 238 us (level)
  Pallas kernels: 152 us -> 147 us
  local copies, waits for them, and re-layouts: 30.9 us -> 35.3 us
    pallas_call x1, Pallas kernels: 77.9 us -> 72.3 us  [reduce_call(): pl.pallas_call(functools.partial(reduce_kernel, cut), out_shape=jax.Shape...]
    unnamed x133 -> x135, local copies, waits for them, and re-layouts: 15.3 us -> 19.7 us
where the time goes in v3:
time: 238 us; the launch traced here: 236 us
  Pallas kernels  147 us (62%)
  local copies, waits for them, and re-layouts  35.3 us (15%)
  matrix products  31.9 us (13%)
  other arithmetic  20.8 us (9%)
    pallas_call x1, Pallas kernels, reduce_call(): pl.pallas_call(functools.partial(reduce_kernel, cut), out_shape=jax.Shape...  72.3 us
    pallas_call x1, Pallas kernels, gather_call(): pl.pallas_call(functools.partial(gather_kernel, cut), out_shape=(jax.Shap...  65.4 us
    unnamed x135, local copies, waits for them, and re-layouts  19.7 us
    dot_general x9, matrix products, against(): lax.dot_general(left, right, (((1,), (1,)), ((), ())), preferred_element_...  11.7 us
    dot_general x9, matrix products, inner_rows(): lax.dot_general(left, right, (((0,), (0,)), ((), ())), preferred_element_...  10.8 us
    dot_general x10, matrix products, product(): return jnp.dot(left, right, preferred_element_type=F32)  9.42 us
    pallas_call x1, Pallas kernels, exchange_call(): pl.pallas_call(exchange_kernel, out_shape=jax.ShapeDtypeStruct(shape, F32...  8.87 us
    slice x2, local copies, waits for them, and re-layouts, body(): every[:, s:s + n].reshape(devices * n, D)  6.01 us

profile of v3, /device:TPU:0, one launch (start us, length us, event | category | flops | bytes accessed | tf_op | source)
XLA Modules:
  0.0 236.4 jit_solution(17801323142415487102)
XLA Ops:
  0.6 0.8 bitcast_dynamic-update-slice_fusion.2
  1.4 0.7 constant_dynamic-update-slice_fusion.4
  2.1 0.7 constant_dynamic-update-slice_fusion.3
  2.8 0.8 constant_dynamic-update-slice_fusion.2
  3.6 0.9 bitcast_dynamic-update-slice_fusion.1
  4.5 0.9 bitcast_dynamic-update-slice_fusion
  5.4 0.9 constant_dynamic-update-slice_fusion.1
  7.0 0.8 pad.18.w_ref
  8.5 1.6 fusion.52.t_ref
  10.1 65.4 %gather_weights.1 = (bf16[32,288,640]{2,1,0:T(8,128)(2,1)}, bf16[4,144,640]{2,1,0:T(8,128)(2,1)}) custom-call(bf16[288,640]{1,0:T(8,128)(2,1)} %pad.18.w_ref, bf16[144,640]{1,0:T(8,128)(2,1)} %fusion.52.t_ref), custom_call_target="tpu_custom_call" | custom-call | tf_op jit(solution)/shard_map/gather_weights/pallas_call | solution.py:211
  75.6 0.9 convert_reduce_fusion
  76.5 1.3 fusion.2
  77.8 1.3 fusion.4
  79.2 0.9 copy-done.25
  80.0 2.1 convolution_convert_fusion.10
  82.2 0.7 slice_convert_fusion.2
  82.9 2.0 fusion.73
  86.8 0.9 multiply_multiply_fusion.4
  87.7 2.2 multiply_reduce_fusion.3
  89.9 2.0 copy.27
  92.0 1.2 multiply_multiply_fusion.3
  93.2 1.9 subtract_convert_fusion.4
  95.1 1.5 fusion.71
  96.7 1.1 multiply_subtract_fusion.1
  97.8 0.7 copy-done.19
  98.5 1.3 fusion.22
  101.1 1.6 fusion.78
  102.7 1.8 copy.28
  104.5 1.4 multiply_reduce_fusion.11
  106.3 4.0 %fusion.72 = (bf16[32,64,640]{2,1,0:T(8,128)(2,1)S(1)}, bf16[32,64,640]{2,1,0:T(8,128)(2,1)S(1)}, bf16[32,64,640]{2,1,0:T(8,128)(2,1)S(1)}) fusion(bf16[32,288,640]{2,1,0:T(8,128)(2,1)} %get-tuple-element.13), kind=kLoop, calls=%fused_computation.193 | loop fusion | bytes 15728640 | tf_op jit(solution)/shard_map/slice | solution.py:420
  110.3 0.9 fusion.79
  111.3 1.0 multiply_convert_fusion.2
  112.3 0.8 copy-done.2
  113.1 0.7 multiply_reduce_fusion.9
  113.8 0.7 fusion.31
  114.5 0.8 fusion.28
  115.3 1.4 multiply_convert_fusion.1
  117.3 0.7 multiply_reduce_fusion.5
  118.1 0.8 multiply_reduce_fusion.6
  120.5 1.6 fusion.14
  122.2 0.8 convolution_multiply_fusion
  123.1 0.7 multiply_reduce_fusion
  124.7 1.4 convolution_convert_fusion.7
  126.1 1.3 convolution_convert_fusion.8
  127.5 8.9 %exchange_keys.1 = f32[128,512]{1,0:T(8,128)S(1)} custom-call(bf16[4,128,512]{2,1,0:T(8,128)(2,1)S(1)} %pad_maximum_fusion.1.g_ref), custom_call_target="tpu_custom_call" | custom-call | tf_op jit(solution)/shard_map/exchange_keys/pallas_call | solution.py:374
  136.4 0.8 fusion.62
  137.5 1.2 convolution_add_fusion.2
  138.7 1.4 fusion.39
  140.1 0.8 fusion.58
  140.9 1.7 fusion.1
  142.8 1.1 fusion.6
  144.0 1.1 fusion.5
  145.1 1.6 fusion
  146.7 0.9 convolution_convert_fusion.2
  147.6 1.8 constant_dynamic-update-slice_fusion.7
  149.4 0.9 convolution_convert_fusion.1
  150.5 1.8 constant_dynamic-update-slice_fusion.6
  152.3 0.9 convolution_convert_fusion
  153.2 1.8 constant_dynamic-update-slice_fusion.5
  156.3 0.9 pad_dynamic-update-slice_fusion.g_ref
  157.2 4.3 %copy-done = bf16[32,288,640]{2,1,0:T(8,128)(2,1)S(1)} copy-done((bf16[32,288,640]{2,1,0:T(8,128)(2,1)S(1)}, bf16[32,288,640]{2,1,0:T(8,128)(2,1)}, u32[]{:S(2)}) %copy-start) | copy-done | bytes 11796504
  161.6 72.3 %reduce_gradients.1 = f32[288,640]{1,0:T(8,128)S(1)} custom-call(bf16[32,288,640]{2,1,0:T(8,128)(2,1)S(1)} %copy-done), custom_call_target="tpu_custom_call" | custom-call | tf_op jit(solution)/shard_map/reduce_gradients/pallas_call | solution.py:325
  234.4 0.7 fusion.75
  235.6 0.8 fusion.74
  (170 shorter events, 10.9 us)
Async XLA Ops:
  5.4 76.7 %copy-start.57 = (s32[1,128]{1,0:T(1,128)S(1)}, s32[1,128]{1,0:T(1,128)}, u32[]{:S(2)}) copy-start(s32[1,128]{1,0:T(1,128)} %param.13) | copy-start | bytes 1540
  79.1 0.9 copy-start.25
  82.1 18.9 %copy-start.43 = (s32[512]{0:T(512)}, s32[512]{0:T(512)S(1)}, u32[]{:S(2)}) copy-start(s32[512]{0:T(512)S(1)} %get-tuple-element.95) | copy-start | bytes 6148
  82.1 18.9 %copy-start.45 = (s32[512]{0:T(512)}, s32[512]{0:T(512)S(1)}, u32[]{:S(2)}) copy-start(s32[512]{0:T(512)S(1)} %get-tuple-element.96) | copy-start | bytes 6148
  82.9 18.2 %copy-start.47 = (s32[4,1,128]{2,1,0:T(1,128)}, s32[4,1,128]{2,1,0:T(1,128)S(1)}, u32[]{:S(2)}) copy-start(s32[4,1,128]{2,1,0:T(1,128)S(1)} %slice_convert_fusion.2) | copy-start | bytes 6148
  82.9 2.0 copy-start.1
  84.8 2.9 %copy-start.26 = (bf16[4,128,640]{2,1,0:T(8,128)(2,1)S(1)}, bf16[4,128,640]{2,1,0:T(8,128)(2,1)}, u32[]{:S(2)}) copy-start(bf16[4,128,640]{2,1,0:T(8,128)(2,1)} %copy-done.25) | copy-start | bytes 1966084
  85.5 0.7 copy-start.39
  86.2 8.9 %copy-start.35 = (f32[256]{0:T(256)}, f32[256]{0:T(256)S(1)}, u32[]{:S(2)}) copy-start(f32[256]{0:T(256)S(1)} %get-tuple-element.63) | copy-start | bytes 3076
  86.2 8.9 %copy-start.37 = (f32[256]{0:T(256)}, f32[256]{0:T(256)S(1)}, u32[]{:S(2)}) copy-start(f32[256]{0:T(256)S(1)} %get-tuple-element.64) | copy-start | bytes 3076
  86.8 8.3 %copy-start.33 = (f32[128,4]{0,1:T(4,128)}, f32[128,4]{0,1:T(4,128)S(1)}, u32[]{:S(2)}) copy-start(f32[128,4]{0,1:T(4,128)S(1)} %get-tuple-element.68) | copy-start | bytes 6148
  92.0 3.1 %copy-start.41 = (f32[512]{0:T(512)}, f32[512]{0:T(512)S(1)}, u32[]{:S(2)}) copy-start(f32[512]{0:T(512)S(1)} %add_rsqrt_fusion) | copy-start | bytes 6148
  96.6 3.7 %copy-start.27 = (f32[128,128]{1,0:T(8,128)}, f32[128,128]{1,0:T(8,128)S(1)}, u32[]{:S(2)}) copy-start(f32[128,128]{1,0:T(8,128)S(1)} %get-tuple-element.29) | copy-start | bytes 196612
  96.6 3.7 %copy-start.58 = (bf16[512,256]{1,0:T(8,128)(2,1)S(1)}, bf16[512,256]{1,0:T(8,128)(2,1)}, u32[]{:S(2)}) copy-start(bf16[512,256]{1,0:T(8,128)(2,1)} %convolution_convert_fusion.10) | copy-start | bytes 786436
  97.8 0.7 copy-start.19
  99.9 1.1 copy-start.17
  99.9 1.1 copy-start.51
  100.3 0.7 copy-start.53
  112.2 0.8 copy-start.2
  112.3 1.5 copy-start.14
  115.3 1.4 copy-start.23
  116.7 1.3 copy-start.10
  116.7 1.3 copy-start.12
  118.1 2.2 copy-start.29
  118.1 2.4 copy-start.18
  118.1 2.4 copy-start.44
  118.1 2.4 copy-start.46
  118.1 2.4 copy-start.48
  118.1 2.4 copy-start.52
  118.1 2.4 copy-start.54
  118.1 2.4 copy-start.59
  118.9 0.7 copy-start.5
  119.7 2.4 %copy-start.15 = (bf16[128,640,1]{1,0,2:T(8,128)(2,1)}, bf16[128,640,1]{1,0,2:T(8,128)(2,1)S(1)}, u32[]{:S(2)}) copy-start(bf16[128,640,1]{1,0,2:T(8,128)(2,1)S(1)} %fusion.57) | copy-start | bytes 491524
  120.2 1.9 copy-start.7
  120.5 1.6 copy-start.31
  120.5 1.6 copy-start.32
  122.1 0.9 copy-start.30
  122.1 0.9 copy-start.34
  122.1 0.9 copy-start.38
  122.2 1.6 copy-start.42
  123.1 1.6 copy-start.8
  123.8 2.3 copy-start.20
  124.2 1.9 copy-start.21
  124.2 12.2 %copy-start.28 = (f32[128,128]{1,0:T(8,128)S(1)}, f32[128,128]{1,0:T(8,128)}, u32[]{:S(2)}) copy-start(f32[128,128]{1,0:T(8,128)} %copy-done.27) | copy-start | bytes 196612
  124.7 12.5 %copy-start.4 = (f32[512,256]{1,0:T(8,128)S(1)}, f32[512,256]{1,0:T(8,128)}, u32[]{:S(2)}) copy-start(f32[512,256]{1,0:T(8,128)} %copy.27) | copy-start | bytes 1572868
  124.7 12.5 %copy-start.36 = (f32[256]{0:T(256)S(1)}, f32[256]{0:T(256)}, u32[]{:S(2)}) copy-start(f32[256]{0:T(256)} %copy-done.35) | copy-start | bytes 3076
  126.1 12.6 %copy-start.40 = (f32[128]{0:T(128)S(1)}, f32[128]{0:T(128)}, u32[]{:S(2)}) copy-start(f32[128]{0:T(128)} %copy-done.39) | copy-start | bytes 1540
  127.4 12.6 %copy-start.6 = (f32[128,640]{1,0:T(8,128)S(1)}, f32[128,640]{1,0:T(8,128)}, u32[]{:S(2)}) copy-start(f32[128,640]{1,0:T(8,128)} %copy-done.5) | copy-start | bytes 983044
  127.5 12.6 %copy-start.56 = (f32[128]{0:T(128)S(1)}, f32[128]{0:T(128)}, u32[]{:S(2)}) copy-start(f32[128]{0:T(128)} %get-tuple-element.69) | copy-start | bytes 1540
  127.5 13.4 %copy-start.22 = (bf16[128,4,256]{0,2,1:T(8,128)(2,1)S(1)}, bf16[128,4,256]{0,2,1:T(8,128)(2,1)}, u32[]{:S(2)}) copy-start(bf16[128,4,256]{0,2,1:T(8,128)(2,1)} %copy-done.21) | copy-start | bytes 786436
  138.7 6.4 %copy-start.9 = (bf16[4,128,256]{1,2,0:T(8,128)(2,1)S(1)}, bf16[4,128,256]{1,2,0:T(8,128)(2,1)}, u32[]{:S(2)}) copy-start(bf16[4,128,256]{1,2,0:T(8,128)(2,1)} %copy.28) | copy-start | bytes 786436
  138.7 6.4 %copy-start.16 = (bf16[128,640,1]{1,0,2:T(8,128)(2,1)S(1)}, bf16[128,640,1]{1,0,2:T(8,128)(2,1)}, u32[]{:S(2)}) copy-start(bf16[128,640,1]{1,0,2:T(8,128)(2,1)} %copy-done.15) | copy-start | bytes 491524
  140.9 5.7 %copy-start.13 = (bf16[128,2048]{1,0:T(8,128)(2,1)S(1)}, bf16[128,2048]{1,0:T(8,128)(2,1)}, u32[]{:S(2)}) copy-start(bf16[128,2048]{1,0:T(8,128)(2,1)} %copy-done.12) | copy-start | bytes 1572868
  147.5 1.9 copy-start.11
  150.3 2.0 copy-start.3
  150.3 2.0 copy-start.24
  153.2 2.0 copy-start.50
  153.2 2.4 %copy-start.49 = (bf16[640]{0:T(1024)(128)(2,1)S(1)}, bf16[640]{0:T(1024)(128)(2,1)}, u32[]{:S(2)}) copy-start(bf16[640]{0:T(1024)(128)(2,1)} %get-tuple-element.22) | copy-start | bytes 3844
  153.2 2.6 %copy-start.55 = (bf16[256]{0:T(256)(128)(2,1)S(1)}, bf16[256]{0:T(256)(128)(2,1)}, u32[]{:S(2)}) copy-start(bf16[256]{0:T(256)(128)(2,1)} %get-tuple-element.14) | copy-start | bytes 1540
  157.2 4.4 %copy-start = (bf16[32,288,640]{2,1,0:T(8,128)(2,1)S(1)}, bf16[32,288,640]{2,1,0:T(8,128)(2,1)}, u32[]{:S(2)}) copy-start(bf16[32,288,640]{2,1,0:T(8,128)(2,1)} %pad_dynamic-update-slice_fusion.g_ref) | copy-start | bytes 35389444
